TPU v7x, 32 devices: a whole 2x2x4 slice. The times are simulated.
32 devices in a mesh: groups: 2 (over x), head: 4 (over y, core), req: 4 (over z).
Axes of the slice: x: 2, y: 2, z: 4, core: 2. Of those that a mesh axis runs over, the one named last changes fastest.
Arguments:
- ssm_input: bfloat16 [16, 64, 4096], P(None, ('groups', 'req'), 'head'), parts along dimension 1, may hold values from -6 to 6
- write_vec: bfloat16 [16, 64, 128], P('head', ('groups', 'req')), parts along dimension 1, may hold values from -6 to 6
- read_vec: bfloat16 [16, 64, 128], P('head', ('groups', 'req')), parts along dimension 1, may hold values from -0.5 to 0.5
- step_raw: float32 [16, 64, 64], P(None, ('groups', 'req'), 'head'), parts along dimension 1, may hold values from -4 to 4
- step_bias: float32 [64], P('head'), may hold values from -3 to -0.5
- decay_rate: float32 [64], P('head'), may hold values from 1 to 16
- skip_gain: float32 [64], P('head'), may hold values from 0.5 to 1.5
- cache_state: bfloat16 [64, 64, 64, 128], P(('groups', 'req'), 'head'), parts along dimension 0, may hold values from -6 to 6
- parents: int32 [64, 16], P(('groups', 'req')), parts along dimension 0, may hold values from -1 to 14, as said below
- out_proj: bfloat16 [4096, 4096], P('head'), may hold values from -0.09375 to 0.09375
- residual: bfloat16 [16, 64, 4096], P('head', ('groups', 'req')), parts along dimension 1, may hold values from -6 to 6
- norm_gain: float32 [4096], replicated, may hold values from 0.1 to 1.9
- router: bfloat16 [4096, 64], replicated, may hold values from -0.09375 to 0.09375
- expert_ids: int32 [16, 64, 10], P('head', ('groups', 'req')), parts along dimension 1, may hold values from 0 to 63, as said below
- gate_proj: bfloat16 [128, 4096, 384], P(('head', 'req')), may hold values from -0.09375 to 0.09375
- up_proj: bfloat16 [128, 4096, 384], P(('head', 'req')), may hold values from -0.09375 to 0.09375
- down_proj: bfloat16 [128, 384, 4096], P(('head', 'req')), may hold values from -0.21875 to 0.21875
Outputs:
- layer_out: bfloat16 [16, 64, 4096], P('head', ('groups', 'req')), parts along dimension 1
There are 2 independent parts, one for each index of `groups`. A program takes and returns all parts, laid end to end along the dimension named above; an argument that names none is the same for every part. Nothing has to cross between parts.
Inputs may be any that keep to these rules, and one draw needn't show every extreme that they name: parents[r, 0] = -1 (the root); for j >= 1, parents[r, j] lies in 0 to j - 1; the last node's parent is node 14. `expert_ids`: each row names 10 different experts. Within the rows of one device (an aligned block of the 4 node index or indices and 8 requests held there) every expert is named by 4 or by 8 rows, 16 experts by 8; one expert is named by 8 rows in every such block.
All inputs are finite; a program needn't handle non-finite values.
Results may differ from a plain program's by a relative error of at most 0.0058.
Values may be sent and summed in bfloat16 or wider, within the bound.
A program may use at most 192 MiB of HBM per device.

v0:
```python
import jax
import jax.numpy as jnp
from jax import lax
from jax.sharding import PartitionSpec as P


def ancestry(parents):
    nodes = parents.shape[1]
    labels = jnp.arange(nodes, dtype=jnp.int32)
    parent_hot = (parents[:, :, None] == labels[None, None, :]).astype(jnp.float32)
    identity = jnp.broadcast_to(jnp.eye(nodes, dtype=jnp.float32), parent_hot.shape)

    def extend(turn, reach):
        return identity + jnp.einsum(
            "rjk,rki->rji", parent_hot, reach, precision=lax.Precision.HIGHEST
        )

    return lax.fori_loop(0, nodes, extend, identity)


def expert_half(rows, gate_proj, up_proj, down_proj):
    gated = jnp.einsum("nhcd,hdf->nhcf", rows, gate_proj, preferred_element_type=jnp.float32)
    lifted = jnp.einsum("nhcd,hdf->nhcf", rows, up_proj, preferred_element_type=jnp.float32)
    act = (jax.nn.silu(gated) * lifted).astype(jnp.bfloat16)
    return jnp.einsum("nhcf,hfd->nhcd", act, down_proj, preferred_element_type=jnp.float32).astype(
        jnp.bfloat16
    )


def send_out(buffer):
    return lax.all_to_all(buffer, ("head", "req"), split_axis=0, concat_axis=0, tiled=True)


def send_back(buffer):
    return lax.all_to_all(buffer, ("head", "req"), split_axis=0, concat_axis=0, tiled=True)


def body(
    ssm_input,
    write_vec,
    read_vec,
    step_raw,
    step_bias,
    decay_rate,
    skip_gain,
    cache_state,
    parents,
    out_proj,
    residual,
    norm_gain,
    router,
    expert_ids,
    gate_proj,
    up_proj,
    down_proj,
):
    nodes, requests, columns = ssm_input.shape
    heads = step_raw.shape[2]
    head_size = columns // heads
    writes, reads = (
        lax.all_gather(write_vec, "head", axis=0, tiled=True),
        lax.all_gather(read_vec, "head", axis=0, tiled=True),
    )
    inputs4 = ssm_input.reshape(nodes, requests, heads, head_size)
    step = jax.nn.softplus(step_raw + step_bias)
    rates = -step * decay_rate
    reach = ancestry(parents)
    depth = jnp.einsum("rji,irh->jrh", reach, rates, precision=lax.Precision.HIGHEST)
    affinity = jnp.einsum("jrn,irn->rji", reads, writes, preferred_element_type=jnp.float32)
    by_request = depth.transpose(1, 0, 2)
    spread = by_request[:, :, None, :] - by_request[:, None, :, :]
    linked = reach[:, :, :, None] > 0
    factor = jnp.where(linked, jnp.exp(jnp.where(linked, spread, 0.0)), 0.0)
    weights = (factor * affinity[:, :, :, None] * step.transpose(1, 0, 2)[:, None, :, :]).astype(
        jnp.bfloat16
    )
    tree_part = jnp.einsum("rjih,irhp->jrhp", weights, inputs4, preferred_element_type=jnp.float32)
    cache_part = jnp.einsum(
        "jrn,rhpn->jrhp", reads, cache_state, preferred_element_type=jnp.float32
    )
    cache_part = cache_part * jnp.exp(depth)[:, :, :, None]
    ssm_out = (tree_part + cache_part + skip_gain[:, None] * inputs4.astype(jnp.float32)).astype(
        jnp.bfloat16
    )
    ssm_out = ssm_out.reshape(nodes, requests, columns)
    local_nodes = residual.shape[0]
    width = residual.shape[2]
    mixed = lax.psum_scatter(
        jnp.einsum("jrk,kd->jrd", ssm_out, out_proj, preferred_element_type=jnp.float32),
        "head",
        scatter_dimension=0,
        tiled=True,
    )
    after_mixer = (residual.astype(jnp.float32) + mixed).astype(jnp.bfloat16)
    widened = after_mixer.astype(jnp.float32)
    meansq = jnp.mean(widened * widened, axis=-1, keepdims=True)
    normed = (widened * lax.rsqrt(meansq + 1e-05) * norm_gain).astype(jnp.bfloat16)
    token_count = local_nodes * requests
    topk = expert_ids.shape[2]
    experts = router.shape[1]
    capacity = 2 * token_count * topk // (experts + experts // 4)
    flat_rows = normed.reshape(token_count, width)
    choices_flat = expert_ids.reshape(token_count, topk)
    expert_labels = jnp.arange(experts, dtype=jnp.int32)
    named = (choices_flat[:, :, None] == expert_labels[None, None, :]).astype(jnp.int32)
    listed = named.reshape(token_count * topk, experts)
    earlier = jnp.cumsum(listed, axis=0) - listed
    slot = jnp.sum(earlier * listed, axis=1).reshape(token_count, topk)
    logits = jnp.dot(flat_rows, router, preferred_element_type=jnp.float32)
    picked_logits = jnp.sum(named.astype(jnp.float32) * logits[:, None, :], axis=2)
    powered = jnp.exp(picked_logits)
    gate = (powered / jnp.sum(powered, axis=1, keepdims=True)).astype(jnp.bfloat16)
    place = choices_flat * capacity + slot
    slot_labels = jnp.arange(experts * capacity, dtype=jnp.int32)
    match = place[:, :, None] == slot_labels[None, None, :]
    selector = jnp.any(match, axis=1).astype(jnp.bfloat16)
    combiner = jnp.sum(jnp.where(match, gate.astype(jnp.float32)[:, :, None], 0.0), axis=1).astype(
        jnp.bfloat16
    )
    dispatch = jnp.einsum(
        "tq,td->qd", selector, flat_rows, preferred_element_type=jnp.float32
    ).astype(jnp.bfloat16)
    device_count = lax.axis_size("head") * lax.axis_size("req")
    held = gate_proj.shape[0]
    doubled = jnp.concatenate([dispatch, dispatch], axis=0).reshape(
        device_count, held, capacity, width
    )
    arrived = send_out(doubled)
    partial_value = expert_half(arrived, gate_proj, up_proj, down_proj)
    returned = send_back(partial_value).reshape(2, experts * capacity, width)
    expert_out = (returned[0].astype(jnp.float32) + returned[1].astype(jnp.float32)).astype(
        jnp.bfloat16
    )
    moe = jnp.dot(combiner, expert_out, preferred_element_type=jnp.float32)
    layer_out = (after_mixer.reshape(token_count, width).astype(jnp.float32) + moe).astype(
        jnp.bfloat16
    )
    return layer_out.reshape(local_nodes, requests, width)


def solution(mesh):
    in_specs = (
        P(None, ("groups", "req"), "head"),
        P("head", ("groups", "req"), None),
        P("head", ("groups", "req"), None),
        P(None, ("groups", "req"), "head"),
        P("head"),
        P("head"),
        P("head"),
        P(("groups", "req"), "head", None, None),
        P(("groups", "req"), None),
        P("head", None),
        P("head", ("groups", "req"), None),
        P(),
        P(),
        P("head", ("groups", "req"), None),
        P(("head", "req"), None, None),
        P(("head", "req"), None, None),
        P(("head", "req"), None, None),
    )
    out_specs = P("head", ("groups", "req"), None)
    return jax.shard_map(body, mesh=mesh, in_specs=in_specs, out_specs=out_specs, check_vma=False)
```

profile of v0, /device:TPU:0, one launch (start us, length us, event | category | flops | bytes accessed | tf_op | source)
XLA Modules:
  0.0 528.0 jit_solution(10458382068559071757)
XLA Ops:
  6.5 0.0 copy-start
  6.5 0.0 reduce-scatter.2.cloned.1.call-start
  6.6 15.9 %while.11 = (s32[]{:T(128)}, f32[8,16,16]{2,1,0:T(8,128)S(1)}, s32[8,16]{1,0:T(8,128)}, f32[16,16]{1,0:T(8,128)S(1)}, s32[]{:T(128)}) while((s32[]{:T(128)}, f32[8,16,16]{2,1,0:T(8,128)S(1)}, s32[8,16]{1,0:T(8,128)}, f32[16,16]{1,0:T(8,128)S(1)}, s32[]{:T(128)}) %tuple.23), condition=%wide.region_1.2_spmd.clone, body=%wide.region_0.1_spmd.clone.sunk | while | flops 399362 | bytes 34365 | solution.py:18
  6.6 1.1 convolution_add_fusion.3
  7.7 0.9 convolution_add_fusion.3
  8.7 0.9 convolution_add_fusion.3
  9.7 0.9 convolution_add_fusion.3
  10.7 0.9 convolution_add_fusion.3
  11.6 0.9 convolution_add_fusion.3
  12.6 0.9 convolution_add_fusion.3
  13.6 0.9 convolution_add_fusion.3
  14.6 0.9 convolution_add_fusion.3
  15.6 0.9 convolution_add_fusion.3
  16.6 0.9 convolution_add_fusion.3
  17.6 0.9 convolution_add_fusion.3
  18.5 0.9 convolution_add_fusion.3
  19.5 0.9 convolution_add_fusion.3
  20.5 0.9 convolution_add_fusion.3
  21.5 0.9 convolution_add_fusion.3
  22.5 0.9 negate_multiply_fusion
  23.4 0.3 fusion.54
  23.7 1.3 reshape.100
  25.0 0.1 copy.48
  25.1 6.4 %all_gather.6 = bf16[16,8,128]{2,1,0:T(8,128)(2,1)S(1)} all-gather(bf16[4,8,128]{2,1,0:T(8,128)(2,1)} %param.21), channel_id=1, replica_groups=mesh['groups'=2,'head'=4,'req'=4] {'head'}, dimensions={0}, use_global_device_ids=true | all-gather | bytes 40960 | tf_op jit(solution)/shard_map/all_gather | solution.py:62
  31.5 5.6 %all_gather.7 = bf16[16,8,128]{2,1,0:T(8,128)(2,1)S(1)} all-gather(bf16[4,8,128]{2,1,0:T(8,128)(2,1)} %param.20), channel_id=1, replica_groups=mesh['groups'=2,'head'=4,'req'=4] {'head'}, dimensions={0}, use_global_device_ids=true | all-gather | bytes 40960 | tf_op jit(solution)/shard_map/all_gather | solution.py:61
  37.1 0.1 fusion.57
  37.3 0.9 convolution_bitcast_fusion.1
  38.1 0.0 copy-done
  38.1 2.4 fusion.35
  40.6 0.0 copy-start.3
  40.6 0.1 copy.52
  40.7 0.0 copy-start.5
  40.7 0.3 reshape.101
  41.1 6.0 %fusion.12 = f32[16,8,4096]{2,1,0:T(8,128)} fusion(bf16[16,8,1024]{2,1,0:T(8,128)(2,1)S(1)} %reshape.101, bf16[1024,4096]{1,0:T(8,128)(2,1)} %param.28), kind=kOutput, calls=%fused_computation.13 | convolution fusion | flops 1073741824 | bytes 10747904 | tf_op jit(solution)/shard_map/jrk,kd->jrd/dot_general | solution.py:89
  47.1 0.0 reduce-scatter.2.cloned.1.call-update
  47.1 0.0 copy-done.4
  47.1 0.1 eq.64
  47.3 0.9 reduce-window.6
  48.2 0.2 slice_reduce_fusion
  48.4 0.1 bitcast_bitcast_fusion
  48.6 0.1 reshape.105
  48.7 0.1 copy.55
  48.8 0.2 fusion.37
  48.9 31.2 %reduce-scatter.2.cloned.1.call-done = f32[4,8,4096]{2,1,0:T(8,128)} async-done(((f32[16,8,4096]{2,1,0:T(8,128)}), f32[4,8,4096]{2,1,0:T(8,128)}) %reduce-scatter.2.cloned.1.call-update) | async-done | bytes 524304 | tf_op jit(solution)/shard_map/reduce_scatter | solution.py:88
  80.2 0.0 copy-done.3
  80.2 1.2 fusion.38
  81.4 0.0 copy-done.5
  81.4 3.3 convolution_convert_fusion
  84.7 7.8 %pad_maximum_fusion = bf16[1024,4096]{1,0:T(8,128)(2,1)} fusion(bf16[512,4096]{1,0:T(8,128)(2,1)} %convolution_convert_fusion), kind=kLoop, calls=%fused_computation.12 | loop fusion | flops 16777216 | bytes 12582912 | tf_op jit(solution)/shard_map/concatenate | solution.py:125
  92.5 189.3 %all_to_all.10 = bf16[16,8,8,4096]{3,2,1,0:T(8,128)(2,1)} all-to-all(bf16[16,8,8,4096]{3,2,1,0:T(8,128)(2,1)} %bitcast.104), channel_id=1, replica_groups=mesh['groups'=2,'head'=4,'req'=4] {'head','req'}, dimensions={0} | all-to-all | bytes 16777216 | tf_op jit(solution)/shard_map/all_to_all | solution.py:31
  281.7 13.0 %fusion.8 = f32[8,16,8,384]{3,2,1,0:T(8,128)S(1)} fusion(bf16[8,4096,384]{2,1,0:T(8,128)(2,1)} %param.34, bf16[16,8,8,4096]{3,2,1,0:T(8,128)(2,1)} %all_to_all.10), kind=kOutput, calls=%fused_computation.8 | convolution fusion | flops 3221225472 | bytes 35127296 | tf_op jit(solution)/shard_map/nhcd,hdf->nhcf/dot_general | solution.py:23
  294.7 23.8 %convert_bitcast_fusion = bf16[16,8,8,4096]{3,2,0,1:T(8,128)(2,1)} fusion(bf16[8,384,4096]{2,1,0:T(8,128)(2,1)} %param.35, f32[8,16,8,384]{3,2,1,0:T(8,128)S(1)} %fusion.8, bf16[8,4096,384]{2,1,0:T(8,128)(2,1)} %param.33, bf16[16,8,8,4096]{3,2,1,0:T(8,128)(2,1)} %all_to_all.10), kind=kOutput, calls=%fused_computation.16 | convolution fusion | flops 6449004544 | bytes 68681728 | tf_op jit(solution)/shard_map/nhcf,hfd->nhcd/dot_general | solution.py:25
  318.5 7.7 %copy.59 = bf16[16,8,8,4096]{3,2,1,0:T(8,128)(2,1)} copy(bf16[16,8,8,4096]{3,2,0,1:T(8,128)(2,1)} %convert_bitcast_fusion) | data formatting | bytes 16777216 | tf_op jit(solution)/shard_map/convert_element_type | solution.py:25
  326.2 4.9 all-to-all-start.1
  331.1 0.1 copy.56
  331.1 0.0 copy-done.2
  331.1 0.3 fusion.50
  331.5 0.2 multiply_reduce_fusion
  331.7 0.0 copy-start.1
  331.7 0.2 select_reduce_fusion
  331.9 183.4 %all-to-all-done.1 = bf16[16,8,8,4096]{3,2,1,0:T(8,128)(2,1)} async-done(((bf16[16,8,8,4096]{3,2,1,0:T(8,128)(2,1)}), bf16[16,8,8,4096]{3,2,1,0:T(8,128)(2,1)}, u32[]{:S(2)}, u32[]{:S(2)}) %all-to-all-start.1) | async-done | bytes 8388640 | tf_op jit(solution)/shard_map/all_to_all | solution.py:35
  515.3 4.3 add_convert_fusion
  519.6 1.5 fusion.19
  521.1 0.0 copy-done.1
  (30 shorter events, 0.3 us)
Async XLA Ops:
  6.5 31.6 %copy-start = (bf16[8,16,64,128]{3,2,1,0:T(8,128)(2,1)S(1)}, bf16[8,16,64,128]{3,2,1,0:T(8,128)(2,1)}, u32[]{:S(2)}) copy-start(bf16[8,16,64,128]{3,2,1,0:T(8,128)(2,1)} %param.26) | copy-start | bytes 6291460
  6.5 73.6 %reduce-scatter.2.cloned.1.call-start = ((), (), s32[]{:S(2)}) async-start(), calls=%async_computation.3 | async-start | bytes 2621440 | tf_op jit(solution)/shard_map/reduce_scatter | solution.py:88
  40.6 6.5 %copy-start.4 = (s32[4,8,10]{2,1,0:T(8,128)S(1)}, s32[4,8,10]{2,1,0:T(8,128)}, u32[]{:S(2)}) copy-start(s32[4,8,10]{2,1,0:T(8,128)} %param.32) | copy-start | bytes 3844
  40.6 39.6 %copy-start.3 = (bf16[4,8,4096]{2,1,0:T(8,128)(2,1)S(1)}, bf16[4,8,4096]{2,1,0:T(8,128)(2,1)}, u32[]{:S(2)}) copy-start(bf16[4,8,4096]{2,1,0:T(8,128)(2,1)} %param.29) | copy-start | bytes 786436
  40.7 40.7 %copy-start.5 = (f32[4096]{0:T(1024)S(1)}, f32[4096]{0:T(1024)}, u32[]{:S(2)}) copy-start(f32[4096]{0:T(1024)} %param.30) | copy-start | bytes 49156
  326.2 5.0 copy-start.2
  326.2 189.1 %all-to-all-start.1 = ((bf16[16,8,8,4096]{3,2,1,0:T(8,128)(2,1)}), bf16[16,8,8,4096]{3,2,1,0:T(8,128)(2,1)}, u32[]{:S(2)}, u32[]{:S(2)}) async-start(bf16[16,8,8,4096]{3,2,1,0:T(8,128)(2,1)} %copy.59), calls=%async_computation.2 | async-start | bytes 16777216 | tf_op jit(solution)/shard_map/all_to_all | solution.py:35
  331.7 189.4 %copy-start.1 = (bf16[8,16,64,128]{3,2,1,0:T(8,128)(2,1)S(1)}, bf16[8,16,64,128]{3,2,1,0:T(8,128)(2,1)}, u32[]{:S(2)}) copy-start(bf16[8,16,64,128]{3,2,1,0:T(8,128)(2,1)} %param.26) | copy-start | bytes 6291460
Sparse Core Ops, SparseCore 0:
  47.2 32.8 reduce-scatter.1
where the time goes:
time: 529 us; the launch traced here: 528 us
  waiting for transfers between devices  215 us (41%)
  blocking collectives  201 us (38%)
  matrix products  66.9 us (13%)
  other arithmetic  15.9 us (3%)
  between operations  13.6 us (3%)
  local copies, waits for them, and re-layouts  10.3 us (2%)
    all_to_all x1, blocking collectives, send_out(): lax.all_to_all(buffer, ('head', 'req'), split_axis=0, concat_axis=0, tile...  189 us
    all_to_all x1, waiting for transfers between devices, send_back(): lax.all_to_all(buffer, ('head', 'req'), split_axis=0, concat_axis=0, tile...  183 us
    reduce_scatter x1, waiting for transfers between devices, body(): lax.psum_scatter(jnp.einsum('jrk,kd->jrd', ssm_out, out_proj, preferred_e...  31.2 us
    dot_general x1, matrix products, expert_half(): jnp.einsum('nhcf,hfd->nhcd', act, down_proj, preferred_element_type=jnp.f...  23.8 us
    dot_general x16, matrix products, extend(): jnp.einsum('rjk,rki->rji', parent_hot, reach, precision=lax.Precision.HIG...  15.3 us
    dot_general x1, matrix products, expert_half(): jnp.einsum('nhcd,hdf->nhcf', rows, up_proj, preferred_element_type=jnp.fl...  13 us
  transfers between devices with their start and end apart: 2, of which 2 were waited for; matrix products, arithmetic and copies ran while one was open for 0% of the time, Pallas kernels for 0%

commit v1 on v0

v1 whole, which is shorter than its diff:
```python
import functools
import jax
import jax.numpy as jnp
from jax import lax
from jax.experimental import pallas as pl
from jax.experimental.pallas import tpu as pltpu
from jax.sharding import PartitionSpec as P

F32 = jnp.float32
BF16 = jnp.bfloat16


def ancestry(parents):
    nodes = parents.shape[1]
    labels = jnp.arange(nodes, dtype=jnp.int32)
    power = (parents[:, :, None] == labels[None, None, :]).astype(BF16)
    reach = power + jnp.eye(nodes, dtype=BF16)
    covered = 2
    while covered < nodes:
        power = jnp.einsum("rjk,rki->rji", power, power, preferred_element_type=F32).astype(BF16)
        reach = reach + jnp.einsum("rjk,rki->rji", power, reach, preferred_element_type=F32).astype(BF16)
        covered *= 2
    return reach.astype(F32)


def remote(src, dst, send, recv, head, req):
    return pltpu.make_async_remote_copy(
        src_ref=src,
        dst_ref=dst,
        send_sem=send,
        recv_sem=recv,
        device_id={"head": head, "req": req},
        device_id_type=pl.DeviceIdType.MESH,
    )


def block_kernel(
    ys, zs, cap, chunks,
    part, res, gain, router, ids, wg_h, wu_h, wd_h,
    out,
    buf, wg, wu, wd, xs, act, cmat, gts, ybuf, pbuf, trecv, ysend, yrecv, zsend, zrecv, mt, ms, my, am,
    mt_s, mt_r, my_s, my_r, az_s, ay_s, at_s, ar, rt_s, rt_r, ry_s, ry_r, rz_s, rz_r, w_s, d_s,
):
    head = lax.axis_index("head")
    z = lax.axis_index("req")
    y = head // 2
    c = head % 2
    t = 1 - c
    twin = y * 2 + t
    rows, width = res.shape
    experts = router.shape[1]
    held, hidden = wg_h.shape[0], wg_h.shape[2]
    slots = wg.shape[0]
    dslots = wd.shape[0]
    tokens = 2 * ys * zs * rows
    cw = width // chunks

    def at_y(d):
        return (y + d) % ys

    flip = 1 - 2 * (2 * z // zs)

    def at_z(d):
        return (z + flip * d + zs) % zs

    def blk(yy, cc, zz):
        return (yy * 2 + cc) * zs + zz

    def load_gu(h, slot):
        return (
            pltpu.make_async_copy(wg_h.at[h], wg.at[slot], w_s.at[slot, 0]),
            pltpu.make_async_copy(wu_h.at[h], wu.at[slot], w_s.at[slot, 1]),
        )

    def load_d(k):
        return pltpu.make_async_copy(
            wd_h.at[:, :, pl.ds(k * cw, cw)], wd.at[k % dslots], d_s.at[k % dslots]
        )

    barrier = pltpu.get_barrier_semaphore()
    pl.semaphore_signal(barrier, inc=1, device_id={"head": twin, "req": z}, device_id_type=pl.DeviceIdType.MESH)
    for d in range(1, ys):
        pl.semaphore_signal(barrier, inc=1, device_id={"head": at_y(d) * 2 + c, "req": z}, device_id_type=pl.DeviceIdType.MESH)
    for d in range(1, zs):
        pl.semaphore_signal(barrier, inc=1, device_id={"head": head, "req": (z + d) % zs}, device_id_type=pl.DeviceIdType.MESH)
    pl.semaphore_wait(barrier, ys + zs - 1)

    pending = []
    twin_parts = []
    for d in [*range(1, ys), 0]:
        cp = remote(part.at[at_y(d), t], mt.at[d], mt_s.at[d], mt_r.at[d], twin, z)
        cp.start()
        twin_parts.append((d, cp))
    for h in range(slots):
        for cp in load_gu(h, h):
            cp.start()
    for k in range(dslots):
        load_d(k).start()
    for d, cp in twin_parts:
        cp.wait_recv()
        if d > 0:
            ms[d] = (part[at_y(d), c] + mt[d]).astype(BF16)
            yc = remote(ms.at[d], my.at[ys - d], my_s.at[d], my_r.at[ys - d], at_y(d) * 2 + c, z)
            yc.start()
            pending.append(yc)
        pending.append(cp)
    mixed = part[y, c] + mt[0]
    for r in range(1, ys):
        remote(ms.at[r], my.at[r], my_s.at[r], my_r.at[r], at_y(r) * 2 + c, z).wait_recv()
        mixed = mixed + my[r].astype(F32)
    after = (res[...].astype(F32) + mixed).astype(BF16)
    am[...] = after
    wide = after.astype(F32)
    meansq = jnp.mean(wide * wide, axis=-1, keepdims=True)
    normed = (wide * lax.rsqrt(meansq + 1e-05) * gain[...]).astype(BF16)
    own = blk(y, c, z)
    buf[own, :, :width] = normed
    logits = jnp.dot(normed, router[...], preferred_element_type=F32)
    lanes = lax.broadcasted_iota(jnp.int32, (rows, experts), 1)
    chosen = ids[...]
    named = lanes == chosen[:, 0:1]
    for k in range(1, ids.shape[1]):
        named = named | (lanes == chosen[:, k : k + 1])
    powered = jnp.where(named, jnp.exp(jnp.where(named, logits, 0.0)), 0.0)
    gate = powered / jnp.sum(powered, axis=1, keepdims=True)
    if experts < 128:
        gate = jnp.concatenate([gate, jnp.zeros((rows, 128 - experts), F32)], axis=1)
    buf[own, :, width:] = gate.astype(BF16)

    def pass_y(b, i):
        for d in range(1, ys):
            s = (d - 1) * zs + i
            cp = remote(buf.at[b], buf.at[b], ay_s.at[s], ar.at[b], at_y(d) * 2 + c, z)
            cp.start()
            pending.append(cp)

    def pass_twin(b, i):
        cp = remote(buf.at[b], buf.at[b], at_s.at[i], ar.at[b], twin, z)
        cp.start()
        pending.append(cp)

    def landed(b):
        remote(buf.at[b], buf.at[b], at_s.at[0], ar.at[b], twin, z).wait_recv()

    pass_y(own, 0)
    for d in range(1, zs):
        cp = remote(buf.at[own], buf.at[own], az_s.at[d], ar.at[own], head, at_z(d))
        cp.start()
        pending.append(cp)
    pass_twin(own, 0)
    for d in range(1, zs):
        b = blk(y, c, at_z(d))
        landed(b)
        pass_y(b, d)
        pass_twin(b, d)
    for e in range(1, ys):
        for d in range(zs):
            b = blk(at_y(e), c, at_z(d))
            landed(b)
            pass_twin(b, e * zs + d)
    for e in range(ys):
        for d in range(zs):
            landed(blk(at_y(e), t, at_z(d)))

    gates = buf[:, :, width:].reshape(tokens, 128)
    first = ((head * zs + z) * held) % experts
    row_of = lax.broadcasted_iota(jnp.int32, (128, 128), 0)
    lane_of = lax.broadcasted_iota(jnp.int32, (128, 128), 1)
    pick = ((lane_of == first + row_of) & (row_of < held)).astype(BF16)
    nt = (((1,), (1,)), ((), ()))
    g = lax.dot_general(gates, pick, nt, preferred_element_type=F32)
    gt = lax.dot_general(pick, gates, nt, preferred_element_type=F32)
    up_t = lax.broadcasted_iota(jnp.int32, (tokens, tokens), 0)
    up_u = lax.broadcasted_iota(jnp.int32, (tokens, tokens), 1)
    before = jnp.where(up_t < up_u, 1.0, 0.0).astype(BF16)
    after_m = jnp.where(up_u < up_t, 1.0, 0.0).astype(BF16)
    on = jnp.where(g > 0, 1.0, 0.0).astype(BF16)
    ont = jnp.where(gt > 0, 1.0, 0.0).astype(BF16)
    rank = jnp.dot(after_m, on, preferred_element_type=F32)
    rankt = jnp.dot(ont, before, preferred_element_type=F32)
    rank = jnp.where(g > 0, rank, -1.0)
    gts[...] = jnp.where(gt > 0, rankt, -1.0)
    slot_lane = lax.broadcasted_iota(jnp.int32, (tokens, cap), 1).astype(F32)
    for h in range(held):
        col = jnp.where(rank[:, h : h + 1] == slot_lane, g[:, h : h + 1], 0.0).astype(BF16)
        cmat[:, :, h * cap : (h + 1) * cap] = col.reshape(2 * ys, zs * rows, cap)

    slot_row = lax.broadcasted_iota(jnp.int32, (cap, tokens), 0).astype(F32)

    def expert(h, carry):
        slot = h % slots
        sel = jnp.where(gts[pl.ds(h, 1), :] == slot_row, 1.0, 0.0).astype(BF16)
        for k in range(chunks):
            cols = slice(k * cw, (k + 1) * cw)
            xs[:, cols] = jnp.dot(
                sel, buf[:, :, cols].reshape(tokens, cw), preferred_element_type=F32
            ).astype(BF16)
        for cp in load_gu(h, slot):
            cp.wait()
        gated = jnp.dot(xs[...], wg[slot], preferred_element_type=F32)
        lifted = jnp.dot(xs[...], wu[slot], preferred_element_type=F32)
        act[h] = (gated / (1.0 + jnp.exp(-gated)) * lifted).astype(BF16)

        @pl.when(h + slots < held)
        def _():
            for cp in load_gu(h + slots, slot):
                cp.start()

        return carry

    lax.fori_loop(0, held, expert, 0)

    def produce(k):
        ks = k % dslots
        load_d(k).wait()

        def down(h, carry):
            at = pl.ds(pl.multiple_of(h * cap, cap), cap)
            ybuf[at, :] = jnp.dot(act[h], wd[ks, h], preferred_element_type=F32).astype(BF16)
            return carry

        lax.fori_loop(0, held, down, 0)
        if k + dslots < chunks:
            load_d(k + dslots).start()

        def mix(i):
            v = jnp.dot(cmat[i], ybuf[...], preferred_element_type=F32).astype(BF16)
            pbuf[k, pl.ds(i * zs, zs)] = v.reshape(zs, rows, cw)

        for e in [*range(1, ys), 0]:
            i = at_y(e) * 2 + t
            mix(i)
            cp = remote(pbuf.at[k, pl.ds(i * zs, zs)], trecv.at[k, e], rt_s.at[k, e], rt_r.at[k, e], twin, z)
            cp.start()
            pending.append(cp)
        for e in [*range(1, ys), 0]:
            mix(at_y(e) * 2 + c)

    def sum_twin(k):
        for e in [*range(1, ys), 0]:
            remote(trecv.at[k, e], trecv.at[k, e], rt_s.at[k, e], rt_r.at[k, e], twin, z).wait_recv()
            i = at_y(e) * 2 + c
            mine = pbuf[k, pl.ds(i * zs, zs)].astype(F32)
            ysend[k, e] = (mine + trecv[k, e].astype(F32)).astype(BF16)
            if e > 0:
                cp = remote(ysend.at[k, e], yrecv.at[k, ys - e], ry_s.at[k, e], ry_r.at[k, ys - e], at_y(e) * 2 + c, z)
                cp.start()
                pending.append(cp)

    def sum_y(k):
        total = ysend[k, 0].astype(F32)
        for e in range(1, ys):
            remote(yrecv.at[k, e], yrecv.at[k, e], ry_s.at[k, e], ry_r.at[k, e], at_y(e) * 2 + c, z).wait_recv()
            total = total + yrecv[k, e].astype(F32)
        zsend[k] = total.astype(BF16)
        for d in range(1, zs):
            zz = (z + d) % zs
            cp = remote(zsend.at[k, zz], zrecv.at[k, zs - d], rz_s.at[k, d], rz_r.at[k, zs - d], head, zz)
            cp.start()
            pending.append(cp)

    def finish(k):
        total = zsend[k, z].astype(F32)
        for d in range(1, zs):
            zz = (z + d) % zs
            remote(zsend.at[k, zz], zrecv.at[k, d], rz_s.at[k, d], rz_r.at[k, d], head, zz).wait_recv()
            total = total + zrecv[k, d].astype(F32)
        cols = slice(k * cw, (k + 1) * cw)
        out[:, cols] = (am[:, cols].astype(F32) + total).astype(BF16)

    for k in range(chunks):
        produce(k)
        if k >= 1:
            sum_twin(k - 1)
        if k >= 3:
            sum_y(k - 3)
    sum_twin(chunks - 1)
    for k in range(max(chunks - 3, 0), chunks):
        sum_y(k)
    for k in range(chunks):
        finish(k)
    for cp in pending:
        cp.wait_send()


def experts_block(mixed, residual, norm_gain, router, ids, gate_proj, up_proj, down_proj, capacity):
    heads = lax.axis_size("head")
    zs = lax.axis_size("req")
    ys = heads // 2
    rows, width = residual.shape
    held, _, hidden = gate_proj.shape
    chunks = 4
    slots = min(3, held)
    dslots = 2
    cw = width // chunks
    blocks = heads * zs
    tokens = blocks * rows
    cap = capacity * blocks
    vmem = pl.BlockSpec(memory_space=pltpu.VMEM)
    hbm = pl.BlockSpec(memory_space=pl.ANY)
    dma = pltpu.SemaphoreType.DMA
    return pl.pallas_call(
        functools.partial(block_kernel, ys, zs, cap, chunks),
        out_shape=jax.ShapeDtypeStruct((rows, width), BF16),
        in_specs=[vmem] * 5 + [hbm] * 3,
        out_specs=vmem,
        scratch_shapes=[
            pltpu.VMEM((blocks, rows, width + 128), BF16),
            pltpu.VMEM((slots, width, hidden), BF16),
            pltpu.VMEM((slots, width, hidden), BF16),
            pltpu.VMEM((dslots, held, hidden, cw), BF16),
            pltpu.VMEM((cap, width), BF16),
            pltpu.VMEM((held, cap, hidden), BF16),
            pltpu.VMEM((heads, zs * rows, held * cap), BF16),
            pltpu.VMEM((128, tokens), F32),
            pltpu.VMEM((held * cap, cw), BF16),
            pltpu.VMEM((chunks, blocks, rows, cw), BF16),
            pltpu.VMEM((chunks, ys, zs, rows, cw), BF16),
            pltpu.VMEM((chunks, ys, zs, rows, cw), BF16),
            pltpu.VMEM((chunks, ys, zs, rows, cw), BF16),
            pltpu.VMEM((chunks, zs, rows, cw), BF16),
            pltpu.VMEM((chunks, zs, rows, cw), BF16),
            pltpu.VMEM((ys, rows, width), F32),
            pltpu.VMEM((ys, rows, width), BF16),
            pltpu.VMEM((ys, rows, width), BF16),
            pltpu.VMEM((rows, width), BF16),
            dma((ys,)), dma((ys,)), dma((ys,)), dma((ys,)),
            dma((zs,)), dma((ys * zs,)), dma((ys * zs,)), dma((blocks,)),
            dma((chunks, ys)), dma((chunks, ys)), dma((chunks, ys)), dma((chunks, ys)),
            dma((chunks, zs)), dma((chunks, zs)),
            dma((slots, 2)), dma((dslots,)),
        ],
        compiler_params=pltpu.CompilerParams(
            collective_id=0, has_side_effects=True, vmem_limit_bytes=62 * 2**20
        ),
    )(
        mixed.reshape(ys, 2, rows, width), residual, norm_gain.reshape(1, width), router, ids,
        gate_proj, up_proj, down_proj,
    )


def body(
    ssm_input,
    write_vec,
    read_vec,
    step_raw,
    step_bias,
    decay_rate,
    skip_gain,
    cache_state,
    parents,
    out_proj,
    residual,
    norm_gain,
    router,
    expert_ids,
    gate_proj,
    up_proj,
    down_proj,
):
    nodes, requests, columns = ssm_input.shape
    heads = step_raw.shape[2]
    head_size = columns // heads
    state = write_vec.shape[2]
    both = lax.all_gather(jnp.concatenate([write_vec, read_vec], axis=2), "head", axis=0, tiled=True)
    writes, reads = both[:, :, :state], both[:, :, state:]
    inputs4 = ssm_input.reshape(nodes, requests, heads, head_size)
    step = jax.nn.softplus(step_raw + step_bias)
    rates = -step * decay_rate
    reach = ancestry(parents)
    depth = jnp.einsum("rji,irh->jrh", reach, rates, precision=lax.Precision.HIGHEST)
    affinity = jnp.einsum("jrn,irn->rji", reads, writes, preferred_element_type=jnp.float32)
    by_request = depth.transpose(1, 0, 2)
    spread = by_request[:, :, None, :] - by_request[:, None, :, :]
    linked = reach[:, :, :, None] > 0
    factor = jnp.where(linked, jnp.exp(jnp.where(linked, spread, 0.0)), 0.0)
    weights = (factor * affinity[:, :, :, None] * step.transpose(1, 0, 2)[:, None, :, :]).astype(
        jnp.bfloat16
    )
    tree_part = jnp.einsum("rjih,irhp->jrhp", weights, inputs4, preferred_element_type=jnp.float32)
    cache_part = jnp.einsum(
        "jrn,rhpn->jrhp", reads, cache_state, preferred_element_type=jnp.float32
    )
    cache_part = cache_part * jnp.exp(depth)[:, :, :, None]
    ssm_out = (tree_part + cache_part + skip_gain[:, None] * inputs4.astype(jnp.float32)).astype(
        jnp.bfloat16
    )
    ssm_out = ssm_out.reshape(nodes, requests, columns)
    local_nodes = residual.shape[0]
    width = residual.shape[2]
    mixed = jnp.einsum("jrk,kd->jrd", ssm_out, out_proj, preferred_element_type=jnp.float32)
    token_count = local_nodes * requests
    experts = router.shape[1]
    topk = expert_ids.shape[2]
    capacity = 2 * token_count * topk // (experts + experts // 4)
    layer_out = experts_block(
        mixed,
        residual.reshape(token_count, width),
        norm_gain,
        router,
        expert_ids.reshape(token_count, topk),
        gate_proj,
        up_proj,
        down_proj,
        capacity,
    )
    return layer_out.reshape(local_nodes, requests, width)


def solution(mesh):
    in_specs = (
        P(None, ("groups", "req"), "head"),
        P("head", ("groups", "req"), None),
        P("head", ("groups", "req"), None),
        P(None, ("groups", "req"), "head"),
        P("head"),
        P("head"),
        P("head"),
        P(("groups", "req"), "head", None, None),
        P(("groups", "req"), None),
        P("head", None),
        P("head", ("groups", "req"), None),
        P(),
        P(),
        P("head", ("groups", "req"), None),
        P(("head", "req"), None, None),
        P(("head", "req"), None, None),
        P(("head", "req"), None, None),
    )
    out_specs = P("head", ("groups", "req"), None)
    return jax.shard_map(body, mesh=mesh, in_specs=in_specs, out_specs=out_specs, check_vma=False)
```

time: 529 us -> 137 us (0.26)
  waiting for transfers between devices: 215 us -> 0 us
  blocking collectives: 201 us -> 6.18 us
  Pallas kernels: 0 us -> 111 us
  matrix products: 66.9 us -> 13 us
  other arithmetic: 15.9 us -> 1.69 us
  between operations: 13.6 us -> 0.09 us
  local copies, waits for them, and re-layouts: 10.3 us -> 4.94 us
    all_to_all x1 -> x0, blocking collectives: 189 us -> none  [send_out(): lax.all_to_all(buffer, ('head', 'req'), split_axis=0, concat_axis=0, tile...]
    all_to_all x1 -> x0, waiting for transfers between devices: 183 us -> none  [send_back(): lax.all_to_all(buffer, ('head', 'req'), split_axis=0, concat_axis=0, tile...]
    pallas_call x0 -> x1, Pallas kernels: none -> 111 us  [experts_block(): pl.pallas_call(functools.partial(block_kernel, ys, zs, cap, chunks), out_...]
    dot_general x21 -> x5, matrix products: 57.2 us -> 2.47 us  [the longest x3 1.37 us: ancestry(): jnp.einsum('rjk,rki->rji', power, reach, preferred_element_type=F32)]
    reduce_scatter x1 -> x0, waiting for transfers between devices: 31.2 us -> none  [body(): lax.psum_scatter(jnp.einsum('jrk,kd->jrd', ssm_out, out_proj, preferred_e...]
    convert_element_type x1 -> x0, local copies, waits for them, and re-layouts: 7.7 us -> none  [expert_half(): jnp.einsum('nhcf,hfd->nhcd', act, down_proj, preferred_element_type=jnp.f...]
    concatenate x1, other arithmetic: 7.8 us -> 0.77 us  [body(): jnp.concatenate([write_vec, read_vec], axis=2)]
    all_gather x2 -> x1, blocking collectives: 12 us -> 6.18 us  [body(): lax.all_gather(jnp.concatenate([write_vec, read_vec], axis=2), 'head', ax...]
  transfers between devices with their start and end apart: 2 -> 0, of which waited for: 2 -> 0; matrix products, arithmetic and copies ran while one was open for 0% -> 0% of each run, Pallas kernels for 0% -> 0%
where the time goes in v1:
time: 137 us; the launch traced here: 136 us
  Pallas kernels  111 us (81%)
  matrix products  13 us (9%)
  blocking collectives  6.18 us (5%)
  local copies, waits for them, and re-layouts  4.94 us (4%)
  other arithmetic  1.69 us (1%)
    pallas_call x1, Pallas kernels, experts_block(): pl.pallas_call(functools.partial(block_kernel, ys, zs, cap, chunks), out_...  111 us
    all_gather x1, blocking collectives, body(): lax.all_gather(jnp.concatenate([write_vec, read_vec], axis=2), 'head', ax...  6.18 us
    dot_general x1, matrix products, body(): jnp.einsum('jrk,kd->jrd', ssm_out, out_proj, preferred_element_type=jnp.f...  5.98 us
    dot_general x1, matrix products, body(): jnp.einsum('jrn,rhpn->jrhp', reads, cache_state, preferred_element_type=j...  3.35 us
    unnamed x4, local copies, waits for them, and re-layouts  3.02 us

profile of v1, /device:TPU:0, one launch (start us, length us, event | category | flops | bytes accessed | tf_op | source)
XLA Modules:
  0.0 136.4 jit_solution(14266085181991161716)
XLA Ops:
  0.0 0.0 copy-start
  0.0 0.8 pad_maximum_fusion
  0.8 1.0 convolution_convert_fusion.5
  1.8 1.0 fusion.8
  2.7 0.1 convolution_convert_fusion.3
  2.9 0.1 fusion.7
  3.0 0.3 convert_compare_fusion
  3.3 6.2 %all_gather.3 = bf16[16,8,256]{2,1,0:T(8,128)(2,1)S(1)} all-gather(bf16[4,8,256]{2,1,0:T(8,128)(2,1)S(1)} %pad_maximum_fusion), channel_id=1, replica_groups=mesh['groups'=2,'head'=4,'req'=4] {'head'}, dimensions={0}, use_global_device_ids=true | all-gather | bytes 81920 | tf_op jit(solution)/shard_map/all_gather | solution.py:365
  9.5 0.1 fusion.21
  9.6 0.9 negate_multiply_fusion
  10.5 0.2 fusion.16
  10.8 0.1 copy.34
  10.9 1.3 reshape.38
  12.2 0.9 convolution_bitcast_fusion.1
  13.1 3.4 %fusion.5 = bf16[16,8,16,64]{3,0,2,1:T(8,128)(2,1)S(1)} fusion(f32[16,8,16,64]{3,0,2,1:T(8,128)S(1)} %convolution_bitcast_fusion.1, bf16[8,16,64,128]{3,2,1,0:T(8,128)(2,1)} %param.24, f32[16]{0:T(128)} %param.23, f32[16,8,16]{0,2,1:T(8,128)S(1)} %exponential_bitcast_fusion, bf16[16,8,16,64]{3,2,1,0:T(8,128)(2,1)S(1)} %reshape.38, ...), kind=kOutput, calls=%fused_computation.7 | convolution fusion | flops 34340864 | bytes 3186752 | tf_op jit(solution)/shard_map/jrn,rhpn->jrhp/dot_general | solution.py:381
  16.4 0.1 copy.37
  16.6 0.3 dot_general.45
  16.9 0.0 copy-done
  16.9 1.3 copy.38.router
  18.3 6.0 %fusion.part = f32[2,2,32,4096]{3,2,1,0:T(8,128)} fusion(bf16[2,2,32,1024]{3,2,1,0:T(8,128)(2,1)S(1)} %dot_general.45, bf16[1024,4096]{1,0:T(8,128)(2,1)} %param.26), kind=kOutput, calls=%fused_computation | convolution fusion | flops 1073741824 | bytes 10747904 | tf_op jit(solution)/shard_map/jrk,kd->jrd/dot_general | solution.py:391
  24.2 110.5 %shard_map.163 = bf16[32,4096]{1,0:T(8,128)(2,1)} custom-call(f32[2,2,32,4096]{3,2,1,0:T(8,128)} %fusion.part, bf16[32,4096]{1,0:T(8,128)(2,1)} %bitcast.45, f32[1,4096]{1,0:T(1,128)} %bitcast.47, bf16[4096,64]{1,0:T(8,128)(2,1)} %copy.38.router, s32[32,10]{1,0:T(8,128)} %bitcast.48, bf16[8,4096,384]{2,1,0:T(8,128)(2,1)} %wg_h.1, ...), custom_call_target="tpu_custom_call" | custom-call | tf_op jit(solution)/shard_map/pallas_call | solution.py:302
  134.8 1.7 %copy.57 = bf16[4,8,4096]{2,1,0:T(8,128)(2,1)} copy(bf16[4,8,4096]{2,1,0:T(8,128)(2,1)} %bitcast.44) | data formatting | bytes 524288
  (3 shorter events, 0.0 us)
Async XLA Ops:
  0.0 16.9 %copy-start = (bf16[4096,64]{0,1:T(8,128)(2,1)S(1)}, bf16[4096,64]{0,1:T(8,128)(2,1)}, u32[]{:S(2)}) copy-start(bf16[4096,64]{0,1:T(8,128)(2,1)} %param.29) | copy-start | bytes 1572868

commit v2 on v1

--- a/solution.py
+++ b/solution.py
@@ -38,7 +38,7 @@
     ys, zs, cap, chunks,
     part, res, gain, router, ids, wg_h, wu_h, wd_h,
     out,
-    buf, wg, wu, wd, xs, act, cmat, gts, ybuf, pbuf, trecv, ysend, yrecv, zsend, zrecv, mt, ms, my, am,
+    buf0, bufn, wg, wu, wd, smat, acc, act, cmat, ybuf, pbuf, trecv, ysend, yrecv, zsend, zrecv, mt, ms, my, am,
     mt_s, mt_r, my_s, my_r, az_s, ay_s, at_s, ar, rt_s, rt_r, ry_s, ry_r, rz_s, rz_r, w_s, d_s,
 ):
     head = lax.axis_index("head")
@@ -48,7 +48,7 @@
     t = 1 - c
     twin = y * 2 + t
     rows, width = res.shape
-    experts = router.shape[1]
+    experts = router.shape[0]
     held, hidden = wg_h.shape[0], wg_h.shape[2]
     slots = wg.shape[0]
     dslots = wd.shape[0]
@@ -66,10 +66,14 @@
     def blk(yy, cc, zz):
         return (yy * 2 + cc) * zs + zz
 
-    def load_gu(h, slot):
+    units = held * chunks
+
+    def load_gu(u):
+        slot = u % slots
+        at = pl.ds(pl.multiple_of((u // held) * cw, cw), cw)
         return (
-            pltpu.make_async_copy(wg_h.at[h], wg.at[slot], w_s.at[slot, 0]),
-            pltpu.make_async_copy(wu_h.at[h], wu.at[slot], w_s.at[slot, 1]),
+            pltpu.make_async_copy(wg_h.at[u % held, at, :], wg.at[slot], w_s.at[slot, 0]),
+            pltpu.make_async_copy(wu_h.at[u % held, at, :], wu.at[slot], w_s.at[slot, 1]),
         )
 
     def load_d(k):
@@ -91,8 +95,8 @@
         cp = remote(part.at[at_y(d), t], mt.at[d], mt_s.at[d], mt_r.at[d], twin, z)
         cp.start()
         twin_parts.append((d, cp))
-    for h in range(slots):
-        for cp in load_gu(h, h):
+    for u in range(slots):
+        for cp in load_gu(jnp.int32(u)):
             cp.start()
     for k in range(dslots):
         load_d(k).start()
@@ -114,8 +118,11 @@
     meansq = jnp.mean(wide * wide, axis=-1, keepdims=True)
     normed = (wide * lax.rsqrt(meansq + 1e-05) * gain[...]).astype(BF16)
     own = blk(y, c, z)
-    buf[own, :, :width] = normed
-    logits = jnp.dot(normed, router[...], preferred_element_type=F32)
+    nt = (((1,), (1,)), ((), ()))
+    buf0[own, :, :cw] = normed[:, :cw]
+    for k in range(1, chunks):
+        bufn[k - 1, own] = normed[:, k * cw : (k + 1) * cw]
+    logits = lax.dot_general(normed, router[...], nt, preferred_element_type=F32)
     lanes = lax.broadcasted_iota(jnp.int32, (rows, experts), 1)
     chosen = ids[...]
     named = lanes == chosen[:, 0:1]
@@ -125,49 +132,98 @@
     gate = powered / jnp.sum(powered, axis=1, keepdims=True)
     if experts < 128:
         gate = jnp.concatenate([gate, jnp.zeros((rows, 128 - experts), F32)], axis=1)
-    buf[own, :, width:] = gate.astype(BF16)
-
-    def pass_y(b, i):
+    buf0[own, :, cw:] = gate.astype(BF16)
+
+    def block(k, b):
+        return buf0.at[b] if k == 0 else bufn.at[k - 1, b]
+
+    def pass_y(k, b, i):
         for d in range(1, ys):
             s = (d - 1) * zs + i
-            cp = remote(buf.at[b], buf.at[b], ay_s.at[s], ar.at[b], at_y(d) * 2 + c, z)
+            cp = remote(block(k, b), block(k, b), ay_s.at[k, s], ar.at[k, b], at_y(d) * 2 + c, z)
             cp.start()
             pending.append(cp)
 
-    def pass_twin(b, i):
-        cp = remote(buf.at[b], buf.at[b], at_s.at[i], ar.at[b], twin, z)
+    def pass_twin(k, b, i):
+        cp = remote(block(k, b), block(k, b), at_s.at[k, i], ar.at[k, b], twin, z)
         cp.start()
         pending.append(cp)
 
-    def landed(b):
-        remote(buf.at[b], buf.at[b], at_s.at[0], ar.at[b], twin, z).wait_recv()
-
-    pass_y(own, 0)
-    for d in range(1, zs):
-        cp = remote(buf.at[own], buf.at[own], az_s.at[d], ar.at[own], head, at_z(d))
-        cp.start()
-        pending.append(cp)
-    pass_twin(own, 0)
-    for d in range(1, zs):
-        b = blk(y, c, at_z(d))
-        landed(b)
-        pass_y(b, d)
-        pass_twin(b, d)
-    for e in range(1, ys):
-        for d in range(zs):
-            b = blk(at_y(e), c, at_z(d))
-            landed(b)
-            pass_twin(b, e * zs + d)
-    for e in range(ys):
-        for d in range(zs):
-            landed(blk(at_y(e), t, at_z(d)))
-
-    gates = buf[:, :, width:].reshape(tokens, 128)
+    def landed(k, b):
+        remote(block(k, b), block(k, b), at_s.at[k, 0], ar.at[k, b], twin, z).wait_recv()
+
+    def send_own(k):
+        pass_y(k, own, 0)
+        for d in range(1, zs):
+            cp = remote(block(k, own), block(k, own), az_s.at[k, d], ar.at[k, own], head, at_z(d))
+            cp.start()
+            pending.append(cp)
+        pass_twin(k, own, 0)
+
+    def relay_z(k):
+        for d in range(1, zs):
+            b = blk(y, c, at_z(d))
+            landed(k, b)
+            pass_y(k, b, d)
+            pass_twin(k, b, d)
+
+    def relay_y(k):
+        for e in range(1, ys):
+            for d in range(zs):
+                b = blk(at_y(e), c, at_z(d))
+                landed(k, b)
+                pass_twin(k, b, e * zs + d)
+
+    def all_in(k):
+        for e in range(ys):
+            for d in range(zs):
+                landed(k, blk(at_y(e), t, at_z(d)))
+
+    def select(k):
+        rows_k = (buf0[:, :, :cw] if k == 0 else bufn[k - 1]).reshape(tokens, cw)
+        half = cw // 2
+        for n in range(2):
+            cols = slice(n * half, (n + 1) * half)
+            ybuf[:, cols] = jnp.dot(smat[...], rows_k[:, cols], preferred_element_type=F32).astype(BF16)
+
+    def apply(k, low, high):
+        def expert(h, carry):
+            u = k * held + h
+            slot = u % slots
+            x = ybuf[pl.ds(pl.multiple_of(h * cap, cap), cap), :]
+            for cp in load_gu(u):
+                cp.wait()
+            gated = jnp.dot(x, wg[slot], preferred_element_type=F32)
+            lifted = jnp.dot(x, wu[slot], preferred_element_type=F32)
+            if k > 0:
+                gated = gated + acc[h, 0]
+                lifted = lifted + acc[h, 1]
+            if k < chunks - 1:
+                acc[h, 0] = gated
+                acc[h, 1] = lifted
+            else:
+                act[h] = (gated / (1.0 + jnp.exp(-gated)) * lifted).astype(BF16)
+
+            @pl.when(u + slots < units)
+            def _():
+                for cp in load_gu(u + slots):
+                    cp.start()
+
+            return carry
+
+        lax.fori_loop(low, high, expert, 0)
+
+    for k in range(chunks):
+        send_own(k)
+    relay_z(0)
+    relay_y(0)
+    all_in(0)
+
+    gates = buf0[:, :, cw:].reshape(tokens, 128)
     first = ((head * zs + z) * held) % experts
     row_of = lax.broadcasted_iota(jnp.int32, (128, 128), 0)
     lane_of = lax.broadcasted_iota(jnp.int32, (128, 128), 1)
     pick = ((lane_of == first + row_of) & (row_of < held)).astype(BF16)
-    nt = (((1,), (1,)), ((), ()))
     g = lax.dot_general(gates, pick, nt, preferred_element_type=F32)
     gt = lax.dot_general(pick, gates, nt, preferred_element_type=F32)
     up_t = lax.broadcasted_iota(jnp.int32, (tokens, tokens), 0)
@@ -179,36 +235,32 @@
     rank = jnp.dot(after_m, on, preferred_element_type=F32)
     rankt = jnp.dot(ont, before, preferred_element_type=F32)
     rank = jnp.where(g > 0, rank, -1.0)
-    gts[...] = jnp.where(gt > 0, rankt, -1.0)
+    rankt = jnp.where(gt > 0, rankt, -1.0)
+    slot_row = lax.broadcasted_iota(jnp.int32, (cap, tokens), 0).astype(F32)
+    for h in range(held):
+        smat[h * cap : (h + 1) * cap, :] = jnp.where(rankt[h : h + 1, :] == slot_row, 1.0, 0.0).astype(BF16)
+    select(0)
+    relay_z(1)
     slot_lane = lax.broadcasted_iota(jnp.int32, (tokens, cap), 1).astype(F32)
     for h in range(held):
         col = jnp.where(rank[:, h : h + 1] == slot_lane, g[:, h : h + 1], 0.0).astype(BF16)
-        cmat[:, :, h * cap : (h + 1) * cap] = col.reshape(2 * ys, zs * rows, cap)
-
-    slot_row = lax.broadcasted_iota(jnp.int32, (cap, tokens), 0).astype(F32)
-
-    def expert(h, carry):
-        slot = h % slots
-        sel = jnp.where(gts[pl.ds(h, 1), :] == slot_row, 1.0, 0.0).astype(BF16)
-        for k in range(chunks):
-            cols = slice(k * cw, (k + 1) * cw)
-            xs[:, cols] = jnp.dot(
-                sel, buf[:, :, cols].reshape(tokens, cw), preferred_element_type=F32
-            ).astype(BF16)
-        for cp in load_gu(h, slot):
-            cp.wait()
-        gated = jnp.dot(xs[...], wg[slot], preferred_element_type=F32)
-        lifted = jnp.dot(xs[...], wu[slot], preferred_element_type=F32)
-        act[h] = (gated / (1.0 + jnp.exp(-gated)) * lifted).astype(BF16)
-
-        @pl.when(h + slots < held)
-        def _():
-            for cp in load_gu(h + slots, slot):
-                cp.start()
-
-        return carry
-
-    lax.fori_loop(0, held, expert, 0)
+        col = col.reshape(ys, 2, zs * rows, cap)
+        for e in range(ys):
+            for cc in range(2):
+                cmat[cc, e * zs * rows : (e + 1) * zs * rows, h * cap : (h + 1) * cap] = col[e, cc]
+
+    middle = held // 2
+    for k in range(chunks):
+        if k > 0:
+            select(k)
+        apply(k, 0, middle)
+        if k + 1 < chunks:
+            relay_y(k + 1)
+        apply(k, middle, held)
+        if k + 2 < chunks:
+            relay_z(k + 2)
+        if k + 1 < chunks:
+            all_in(k + 1)
 
     def produce(k):
         ks = k % dslots
@@ -223,24 +275,21 @@
         if k + dslots < chunks:
             load_d(k + dslots).start()
 
-        def mix(i):
-            v = jnp.dot(cmat[i], ybuf[...], preferred_element_type=F32).astype(BF16)
-            pbuf[k, pl.ds(i * zs, zs)] = v.reshape(zs, rows, cw)
-
+        def mix(cc):
+            v = jnp.dot(cmat[cc], ybuf[...], preferred_element_type=F32).astype(BF16)
+            pbuf[k, cc] = v.reshape(ys, zs, rows, cw)
+
+        mix(t)
         for e in [*range(1, ys), 0]:
-            i = at_y(e) * 2 + t
-            mix(i)
-            cp = remote(pbuf.at[k, pl.ds(i * zs, zs)], trecv.at[k, e], rt_s.at[k, e], rt_r.at[k, e], twin, z)
+            cp = remote(pbuf.at[k, t, at_y(e)], trecv.at[k, e], rt_s.at[k, e], rt_r.at[k, e], twin, z)
             cp.start()
             pending.append(cp)
-        for e in [*range(1, ys), 0]:
-            mix(at_y(e) * 2 + c)
+        mix(c)
 
     def sum_twin(k):
         for e in [*range(1, ys), 0]:
             remote(trecv.at[k, e], trecv.at[k, e], rt_s.at[k, e], rt_r.at[k, e], twin, z).wait_recv()
-            i = at_y(e) * 2 + c
-            mine = pbuf[k, pl.ds(i * zs, zs)].astype(F32)
+            mine = pbuf[k, c, at_y(e)].astype(F32)
             ysend[k, e] = (mine + trecv[k, e].astype(F32)).astype(BF16)
             if e > 0:
                 cp = remote(ysend.at[k, e], yrecv.at[k, ys - e], ry_s.at[k, e], ry_r.at[k, ys - e], at_y(e) * 2 + c, z)
@@ -290,7 +339,7 @@
     rows, width = residual.shape
     held, _, hidden = gate_proj.shape
     chunks = 4
-    slots = min(3, held)
+    slots = min(12, held * 4)
     dslots = 2
     cw = width // chunks
     blocks = heads * zs
@@ -305,16 +354,17 @@
         in_specs=[vmem] * 5 + [hbm] * 3,
         out_specs=vmem,
         scratch_shapes=[
-            pltpu.VMEM((blocks, rows, width + 128), BF16),
-            pltpu.VMEM((slots, width, hidden), BF16),
-            pltpu.VMEM((slots, width, hidden), BF16),
+            pltpu.VMEM((blocks, rows, cw + 128), BF16),
+            pltpu.VMEM((chunks - 1, blocks, rows, cw), BF16),
+            pltpu.VMEM((slots, cw, hidden), BF16),
+            pltpu.VMEM((slots, cw, hidden), BF16),
             pltpu.VMEM((dslots, held, hidden, cw), BF16),
-            pltpu.VMEM((cap, width), BF16),
+            pltpu.VMEM((held * cap, tokens), BF16),
+            pltpu.VMEM((held, 2, cap, hidden), F32),
             pltpu.VMEM((held, cap, hidden), BF16),
-            pltpu.VMEM((heads, zs * rows, held * cap), BF16),
-            pltpu.VMEM((128, tokens), F32),
+            pltpu.VMEM((2, ys * zs * rows, held * cap), BF16),
             pltpu.VMEM((held * cap, cw), BF16),
-            pltpu.VMEM((chunks, blocks, rows, cw), BF16),
+            pltpu.VMEM((chunks, 2, ys, zs, rows, cw), BF16),
             pltpu.VMEM((chunks, ys, zs, rows, cw), BF16),
             pltpu.VMEM((chunks, ys, zs, rows, cw), BF16),
             pltpu.VMEM((chunks, ys, zs, rows, cw), BF16),
@@ -325,7 +375,7 @@
             pltpu.VMEM((ys, rows, width), BF16),
             pltpu.VMEM((rows, width), BF16),
             dma((ys,)), dma((ys,)), dma((ys,)), dma((ys,)),
-            dma((zs,)), dma((ys * zs,)), dma((ys * zs,)), dma((blocks,)),
+            dma((chunks, zs)), dma((chunks, ys * zs)), dma((chunks, ys * zs)), dma((chunks, blocks)),
             dma((chunks, ys)), dma((chunks, ys)), dma((chunks, ys)), dma((chunks, ys)),
             dma((chunks, zs)), dma((chunks, zs)),
             dma((slots, 2)), dma((dslots,)),
@@ -334,7 +384,7 @@
             collective_id=0, has_side_effects=True, vmem_limit_bytes=62 * 2**20
         ),
     )(
-        mixed.reshape(ys, 2, rows, width), residual, norm_gain.reshape(1, width), router, ids,
+        mixed.reshape(ys, 2, rows, width), residual, norm_gain.reshape(1, width), router.T, ids,
         gate_proj, up_proj, down_proj,
     )
 

time: 137 us -> 126 us (0.920)
  Pallas kernels: 111 us -> 101 us
    pallas_call x1, Pallas kernels: 111 us -> 101 us  [experts_block(): pl.pallas_call(functools.partial(block_kernel, ys, zs, cap, chunks), out_...]
    unnamed x4 -> x1, local copies, waits for them, and re-layouts: 3.02 us -> 1.67 us
where the time goes in v2:
time: 126 us; the launch traced here: 125 us
  Pallas kernels  101 us (80%)
  matrix products  13 us (10%)
  blocking collectives  6.18 us (5%)
  local copies, waits for them, and re-layouts  3.59 us (3%)
  other arithmetic  1.63 us (1%)
    pallas_call x1, Pallas kernels, experts_block(): pl.pallas_call(functools.partial(block_kernel, ys, zs, cap, chunks), out_...  101 us
    all_gather x1, blocking collectives, body(): lax.all_gather(jnp.concatenate([write_vec, read_vec], axis=2), 'head', ax...  6.18 us
    dot_general x1, matrix products, body(): jnp.einsum('jrk,kd->jrd', ssm_out, out_proj, preferred_element_type=jnp.f...  5.99 us
    dot_general x1, matrix products, body(): jnp.einsum('jrn,rhpn->jrhp', reads, cache_state, preferred_element_type=j...  3.35 us

profile of v2, /device:TPU:0, one launch (start us, length us, event | category | flops | bytes accessed | tf_op | source)
XLA Modules:
  0.0 125.4 jit_solution(5953620342717532091)
XLA Ops:
  0.0 0.7 pad_maximum_fusion
  0.7 1.0 convolution_convert_fusion.5
  1.7 1.0 fusion.8
  2.7 0.1 convolution_convert_fusion.3
  2.8 0.1 fusion.7
  3.0 0.3 convert_compare_fusion
  3.2 6.2 %all_gather.3 = bf16[16,8,256]{2,1,0:T(8,128)(2,1)S(1)} all-gather(bf16[4,8,256]{2,1,0:T(8,128)(2,1)S(1)} %pad_maximum_fusion), channel_id=1, replica_groups=mesh['groups'=2,'head'=4,'req'=4] {'head'}, dimensions={0}, use_global_device_ids=true | all-gather | bytes 81920 | tf_op jit(solution)/shard_map/all_gather | solution.py:415
  9.4 0.1 fusion.21
  9.5 0.9 negate_multiply_fusion
  10.4 0.2 fusion.16
  10.7 0.1 copy.32
  10.8 1.3 %reshape.38 = bf16[16,8,16,64]{3,2,1,0:T(8,128)(2,1)S(1)} reshape(bf16[16,8,1024]{2,1,0:T(8,128)(2,1)} %param.17) | data formatting | bytes 524288 | tf_op jit(solution)/shard_map/reshape | solution.py:417
  12.1 0.9 convolution_bitcast_fusion.1
  13.0 3.4 %fusion.5 = bf16[16,8,16,64]{3,0,2,1:T(8,128)(2,1)S(1)} fusion(f32[16,8,16,64]{3,0,2,1:T(8,128)S(1)} %convolution_bitcast_fusion.1, bf16[8,16,64,128]{3,2,1,0:T(8,128)(2,1)} %param.24, f32[16]{0:T(128)} %param.23, f32[16,8,16]{0,2,1:T(8,128)S(1)} %exponential_bitcast_fusion, bf16[16,8,16,64]{3,2,1,0:T(8,128)(2,1)S(1)} %reshape.38, ...), kind=kOutput, calls=%fused_computation.7 | convolution fusion | flops 34340864 | bytes 3186752 | tf_op jit(solution)/shard_map/jrn,rhpn->jrhp/dot_general | solution.py:431
  16.4 0.1 copy.35
  16.5 0.3 dot_general.45
  16.8 6.0 %fusion.part = f32[2,2,32,4096]{3,2,1,0:T(8,128)} fusion(bf16[2,2,32,1024]{3,2,1,0:T(8,128)(2,1)S(1)} %dot_general.45, bf16[1024,4096]{1,0:T(8,128)(2,1)} %param.26), kind=kOutput, calls=%fused_computation | convolution fusion | flops 1073741824 | bytes 10747904 | tf_op jit(solution)/shard_map/jrk,kd->jrd/dot_general | solution.py:441
  22.8 100.9 %shard_map.163 = bf16[32,4096]{1,0:T(8,128)(2,1)} custom-call(f32[2,2,32,4096]{3,2,1,0:T(8,128)} %fusion.part, bf16[32,4096]{1,0:T(8,128)(2,1)} %bitcast.47, f32[1,4096]{1,0:T(1,128)} %bitcast.49, bf16[64,4096]{1,0:T(8,128)(2,1)} %bitcast.46, s32[32,10]{1,0:T(8,128)} %bitcast.50, bf16[8,4096,384]{2,1,0:T(8,128)(2,1)} %wg_h.1, bf16[8,4096,384]{2,1,0:T(8,128)(2,1)} %wu_h.1, ...), custom_call_target="tpu_custom_call" | custom-call | tf_op jit(solution)/shard_map/pallas_call | solution.py:351
  123.7 1.7 %copy.54 = bf16[4,8,4096]{2,1,0:T(8,128)(2,1)} copy(bf16[4,8,4096]{2,1,0:T(8,128)(2,1)} %bitcast.45) | data formatting | bytes 524288
  (3 shorter events, 0.0 us)

commit v3 on v2

--- a/solution.py
+++ b/solution.py
@@ -35,11 +35,11 @@
 
 
 def block_kernel(
-    ys, zs, cap, chunks,
-    part, res, gain, router, ids, wg_h, wu_h, wd_h,
+    ys, zs, cap, chunks, backs,
+    ssm, proj_h, res, gain, router, ids, wg_h, wu_h, wd_h,
     out,
-    buf0, bufn, wg, wu, wd, smat, acc, act, cmat, ybuf, pbuf, trecv, ysend, yrecv, zsend, zrecv, mt, ms, my, am,
-    mt_s, mt_r, my_s, my_r, az_s, ay_s, at_s, ar, rt_s, rt_r, ry_s, ry_r, rz_s, rz_r, w_s, d_s,
+    part, proj, buf0, bufn, wgu, wd, smat, acc, act, cmat, ybuf, pbuf, trecv, ysend, yrecv, zsend, zrecv, mt, ms, my, am,
+    p_s, mt_s, mt_r, my_s, my_r, az_s, ay_s, at_s, ar, atr, rt_s, rt_r, ry_s, ry_r, rz_s, rz_r, w_s, d_s,
 ):
     head = lax.axis_index("head")
     z = lax.axis_index("req")
@@ -50,10 +50,11 @@
     rows, width = res.shape
     experts = router.shape[0]
     held, hidden = wg_h.shape[0], wg_h.shape[2]
-    slots = wg.shape[0]
+    slots = wgu.shape[0]
     dslots = wd.shape[0]
     tokens = 2 * ys * zs * rows
     cw = width // chunks
+    rw = width // backs
 
     def at_y(d):
         return (y + d) % ys
@@ -72,14 +73,25 @@
         slot = u % slots
         at = pl.ds(pl.multiple_of((u // held) * cw, cw), cw)
         return (
-            pltpu.make_async_copy(wg_h.at[u % held, at, :], wg.at[slot], w_s.at[slot, 0]),
-            pltpu.make_async_copy(wu_h.at[u % held, at, :], wu.at[slot], w_s.at[slot, 1]),
+            pltpu.make_async_copy(wg_h.at[u % held, at, :], wgu.at[slot, :, pl.ds(0, hidden)], w_s.at[slot, 0]),
+            pltpu.make_async_copy(wu_h.at[u % held, at, :], wgu.at[slot, :, pl.ds(hidden, hidden)], w_s.at[slot, 1]),
         )
 
     def load_d(k):
         return pltpu.make_async_copy(
-            wd_h.at[:, :, pl.ds(k * cw, cw)], wd.at[k % dslots], d_s.at[k % dslots]
+            wd_h.at[:, :, pl.ds(k * rw, rw)], wd.at[k % dslots], d_s.at[k % dslots]
         )
+
+    def load_p(k):
+        return pltpu.make_async_copy(proj_h.at[:, pl.ds(k * cw, cw)], proj.at[k % 2], p_s.at[k % 2])
+
+    load_p(0).start()
+    load_p(1).start()
+    for u in range(slots):
+        for cp in load_gu(jnp.int32(u)):
+            cp.start()
+    for k in range(dslots):
+        load_d(k).start()
 
     barrier = pltpu.get_barrier_semaphore()
     pl.semaphore_signal(barrier, inc=1, device_id={"head": twin, "req": z}, device_id_type=pl.DeviceIdType.MESH)
@@ -90,28 +102,40 @@
     pl.semaphore_wait(barrier, ys + zs - 1)
 
     pending = []
-    twin_parts = []
-    for d in [*range(1, ys), 0]:
-        cp = remote(part.at[at_y(d), t], mt.at[d], mt_s.at[d], mt_r.at[d], twin, z)
-        cp.start()
-        twin_parts.append((d, cp))
-    for u in range(slots):
-        for cp in load_gu(jnp.int32(u)):
-            cp.start()
-    for k in range(dslots):
-        load_d(k).start()
-    for d, cp in twin_parts:
-        cp.wait_recv()
-        if d > 0:
-            ms[d] = (part[at_y(d), c] + mt[d]).astype(BF16)
-            yc = remote(ms.at[d], my.at[ys - d], my_s.at[d], my_r.at[ys - d], at_y(d) * 2 + c, z)
-            yc.start()
-            pending.append(yc)
-        pending.append(cp)
-    mixed = part[y, c] + mt[0]
-    for r in range(1, ys):
-        remote(ms.at[r], my.at[r], my_s.at[r], my_r.at[r], at_y(r) * 2 + c, z).wait_recv()
-        mixed = mixed + my[r].astype(F32)
+
+    def mixer(k):
+        load_p(k).wait()
+        v = jnp.dot(ssm[...], proj[k % 2], preferred_element_type=F32)
+        part[k] = v.reshape(ys, 2, rows, cw)
+        if k + 2 < chunks:
+            load_p(k + 2).start()
+        for d in [*range(1, ys), 0]:
+            cp = remote(part.at[k, at_y(d), t], mt.at[k, d], mt_s.at[k, d], mt_r.at[k, d], twin, z)
+            cp.start()
+            pending.append(cp)
+
+    def mixer_y(k):
+        for d in range(1, ys):
+            remote(mt.at[k, d], mt.at[k, d], mt_s.at[k, d], mt_r.at[k, d], twin, z).wait_recv()
+            ms[k, d] = (part[k, at_y(d), c] + mt[k, d]).astype(BF16)
+            cp = remote(ms.at[k, d], my.at[k, ys - d], my_s.at[k, d], my_r.at[k, ys - d], at_y(d) * 2 + c, z)
+            cp.start()
+            pending.append(cp)
+
+    for k in range(chunks):
+        mixer(k)
+        if k > 0:
+            mixer_y(k - 1)
+    mixer_y(chunks - 1)
+    sums = []
+    for k in range(chunks):
+        remote(mt.at[k, 0], mt.at[k, 0], mt_s.at[k, 0], mt_r.at[k, 0], twin, z).wait_recv()
+        total = part[k, y, c] + mt[k, 0]
+        for r in range(1, ys):
+            remote(ms.at[k, r], my.at[k, r], my_s.at[k, r], my_r.at[k, r], at_y(r) * 2 + c, z).wait_recv()
+            total = total + my[k, r].astype(F32)
+        sums.append(total)
+    mixed = jnp.concatenate(sums, axis=1)
     after = (res[...].astype(F32) + mixed).astype(BF16)
     am[...] = after
     wide = after.astype(F32)
@@ -144,40 +168,42 @@
             cp.start()
             pending.append(cp)
 
-    def pass_twin(k, b, i):
-        cp = remote(block(k, b), block(k, b), at_s.at[k, i], ar.at[k, b], twin, z)
+    def pass_twin(k, e):
+        at = pl.ds(blk(at_y(e), c, 0), zs)
+        ref = buf0.at[at] if k == 0 else bufn.at[k - 1, at]
+        cp = remote(ref, ref, at_s.at[k, e], atr.at[k, e], twin, z)
         cp.start()
         pending.append(cp)
 
     def landed(k, b):
         remote(block(k, b), block(k, b), at_s.at[k, 0], ar.at[k, b], twin, z).wait_recv()
 
-    def send_own(k):
-        pass_y(k, own, 0)
+    def send_z(k):
         for d in range(1, zs):
             cp = remote(block(k, own), block(k, own), az_s.at[k, d], ar.at[k, own], head, at_z(d))
             cp.start()
             pending.append(cp)
-        pass_twin(k, own, 0)
 
     def relay_z(k):
         for d in range(1, zs):
             b = blk(y, c, at_z(d))
             landed(k, b)
             pass_y(k, b, d)
-            pass_twin(k, b, d)
+        pass_twin(k, 0)
+        if k + 2 < chunks:
+            pass_y(k + 2, own, 0)
 
     def relay_y(k):
         for e in range(1, ys):
             for d in range(zs):
-                b = blk(at_y(e), c, at_z(d))
-                landed(k, b)
-                pass_twin(k, b, e * zs + d)
+                landed(k, blk(at_y(e), c, at_z(d)))
+            pass_twin(k, e)
 
     def all_in(k):
         for e in range(ys):
-            for d in range(zs):
-                landed(k, blk(at_y(e), t, at_z(d)))
+            at = pl.ds(blk(at_y(e), t, 0), zs)
+            ref = buf0.at[at] if k == 0 else bufn.at[k - 1, at]
+            remote(ref, ref, at_s.at[k, e], atr.at[k, e], twin, z).wait_recv()
 
     def select(k):
         rows_k = (buf0[:, :, :cw] if k == 0 else bufn[k - 1]).reshape(tokens, cw)
@@ -193,16 +219,14 @@
             x = ybuf[pl.ds(pl.multiple_of(h * cap, cap), cap), :]
             for cp in load_gu(u):
                 cp.wait()
-            gated = jnp.dot(x, wg[slot], preferred_element_type=F32)
-            lifted = jnp.dot(x, wu[slot], preferred_element_type=F32)
+            both = jnp.dot(x, wgu[slot], preferred_element_type=F32)
             if k > 0:
-                gated = gated + acc[h, 0]
-                lifted = lifted + acc[h, 1]
+                both = both + acc[h]
             if k < chunks - 1:
-                acc[h, 0] = gated
-                acc[h, 1] = lifted
+                acc[h] = both
             else:
-                act[h] = (gated / (1.0 + jnp.exp(-gated)) * lifted).astype(BF16)
+                gated = both[:, :hidden]
+                act[h] = (gated / (1.0 + jnp.exp(-gated)) * both[:, hidden:]).astype(BF16)
 
             @pl.when(u + slots < units)
             def _():
@@ -214,7 +238,9 @@
         lax.fori_loop(low, high, expert, 0)
 
     for k in range(chunks):
-        send_own(k)
+        if k < 2:
+            pass_y(k, own, 0)
+        send_z(k)
     relay_z(0)
     relay_y(0)
     all_in(0)
@@ -268,16 +294,16 @@
 
         def down(h, carry):
             at = pl.ds(pl.multiple_of(h * cap, cap), cap)
-            ybuf[at, :] = jnp.dot(act[h], wd[ks, h], preferred_element_type=F32).astype(BF16)
+            ybuf[at, :rw] = jnp.dot(act[h], wd[ks, h], preferred_element_type=F32).astype(BF16)
             return carry
 
         lax.fori_loop(0, held, down, 0)
-        if k + dslots < chunks:
+        if k + dslots < backs:
             load_d(k + dslots).start()
 
         def mix(cc):
-            v = jnp.dot(cmat[cc], ybuf[...], preferred_element_type=F32).astype(BF16)
-            pbuf[k, cc] = v.reshape(ys, zs, rows, cw)
+            v = jnp.dot(cmat[cc], ybuf[:, :rw], preferred_element_type=F32).astype(BF16)
+            pbuf[k, cc] = v.reshape(ys, zs, rows, rw)
 
         mix(t)
         for e in [*range(1, ys), 0]:
@@ -314,34 +340,41 @@
             zz = (z + d) % zs
             remote(zsend.at[k, zz], zrecv.at[k, d], rz_s.at[k, d], rz_r.at[k, d], head, zz).wait_recv()
             total = total + zrecv[k, d].astype(F32)
-        cols = slice(k * cw, (k + 1) * cw)
+        cols = slice(k * rw, (k + 1) * rw)
         out[:, cols] = (am[:, cols].astype(F32) + total).astype(BF16)
 
-    for k in range(chunks):
+    for k in range(backs):
         produce(k)
-        if k >= 1:
+        if k < 2:
+            sum_twin(k)
+        elif k > 2:
             sum_twin(k - 1)
-        if k >= 3:
-            sum_y(k - 3)
-    sum_twin(chunks - 1)
-    for k in range(max(chunks - 3, 0), chunks):
+        if k >= 4:
+            sum_y(k - 4)
+        if k >= 6:
+            finish(k - 6)
+    sum_twin(backs - 1)
+    for k in range(backs - 4, backs):
         sum_y(k)
-    for k in range(chunks):
-        finish(k)
+        finish(k - 2)
+    finish(backs - 2)
+    finish(backs - 1)
     for cp in pending:
         cp.wait_send()
 
 
-def experts_block(mixed, residual, norm_gain, router, ids, gate_proj, up_proj, down_proj, capacity):
+def experts_block(ssm_out, out_proj, residual, norm_gain, router, ids, gate_proj, up_proj, down_proj, capacity):
     heads = lax.axis_size("head")
     zs = lax.axis_size("req")
     ys = heads // 2
     rows, width = residual.shape
     held, _, hidden = gate_proj.shape
     chunks = 4
-    slots = min(12, held * 4)
-    dslots = 2
+    backs = 8
+    slots = min(8, held * chunks)
+    dslots = 4
     cw = width // chunks
+    rw = width // backs
     blocks = heads * zs
     tokens = blocks * rows
     cap = capacity * blocks
@@ -349,42 +382,43 @@
     hbm = pl.BlockSpec(memory_space=pl.ANY)
     dma = pltpu.SemaphoreType.DMA
     return pl.pallas_call(
-        functools.partial(block_kernel, ys, zs, cap, chunks),
+        functools.partial(block_kernel, ys, zs, cap, chunks, backs),
         out_shape=jax.ShapeDtypeStruct((rows, width), BF16),
-        in_specs=[vmem] * 5 + [hbm] * 3,
+        in_specs=[vmem, hbm] + [vmem] * 4 + [hbm] * 3,
         out_specs=vmem,
         scratch_shapes=[
+            pltpu.VMEM((chunks, ys, 2, rows, cw), F32),
+            pltpu.VMEM((2, ssm_out.shape[1], cw), BF16),
             pltpu.VMEM((blocks, rows, cw + 128), BF16),
             pltpu.VMEM((chunks - 1, blocks, rows, cw), BF16),
-            pltpu.VMEM((slots, cw, hidden), BF16),
-            pltpu.VMEM((slots, cw, hidden), BF16),
-            pltpu.VMEM((dslots, held, hidden, cw), BF16),
+            pltpu.VMEM((slots, cw, 2 * hidden), BF16),
+            pltpu.VMEM((dslots, held, hidden, rw), BF16),
             pltpu.VMEM((held * cap, tokens), BF16),
-            pltpu.VMEM((held, 2, cap, hidden), F32),
+            pltpu.VMEM((held, cap, 2 * hidden), F32),
             pltpu.VMEM((held, cap, hidden), BF16),
             pltpu.VMEM((2, ys * zs * rows, held * cap), BF16),
             pltpu.VMEM((held * cap, cw), BF16),
-            pltpu.VMEM((chunks, 2, ys, zs, rows, cw), BF16),
-            pltpu.VMEM((chunks, ys, zs, rows, cw), BF16),
-            pltpu.VMEM((chunks, ys, zs, rows, cw), BF16),
-            pltpu.VMEM((chunks, ys, zs, rows, cw), BF16),
-            pltpu.VMEM((chunks, zs, rows, cw), BF16),
-            pltpu.VMEM((chunks, zs, rows, cw), BF16),
-            pltpu.VMEM((ys, rows, width), F32),
-            pltpu.VMEM((ys, rows, width), BF16),
-            pltpu.VMEM((ys, rows, width), BF16),
+            pltpu.VMEM((backs, 2, ys, zs, rows, rw), BF16),
+            pltpu.VMEM((backs, ys, zs, rows, rw), BF16),
+            pltpu.VMEM((backs, ys, zs, rows, rw), BF16),
+            pltpu.VMEM((backs, ys, zs, rows, rw), BF16),
+            pltpu.VMEM((backs, zs, rows, rw), BF16),
+            pltpu.VMEM((backs, zs, rows, rw), BF16),
+            pltpu.VMEM((chunks, ys, rows, cw), F32),
+            pltpu.VMEM((chunks, ys, rows, cw), BF16),
+            pltpu.VMEM((chunks, ys, rows, cw), BF16),
             pltpu.VMEM((rows, width), BF16),
-            dma((ys,)), dma((ys,)), dma((ys,)), dma((ys,)),
-            dma((chunks, zs)), dma((chunks, ys * zs)), dma((chunks, ys * zs)), dma((chunks, blocks)),
-            dma((chunks, ys)), dma((chunks, ys)), dma((chunks, ys)), dma((chunks, ys)),
-            dma((chunks, zs)), dma((chunks, zs)),
+            dma((2,)), dma((chunks, ys)), dma((chunks, ys)), dma((chunks, ys)), dma((chunks, ys)),
+            dma((chunks, zs)), dma((chunks, ys * zs)), dma((chunks, ys)), dma((chunks, blocks)), dma((chunks, ys)),
+            dma((backs, ys)), dma((backs, ys)), dma((backs, ys)), dma((backs, ys)),
+            dma((backs, zs)), dma((backs, zs)),
             dma((slots, 2)), dma((dslots,)),
         ],
         compiler_params=pltpu.CompilerParams(
             collective_id=0, has_side_effects=True, vmem_limit_bytes=62 * 2**20
         ),
     )(
-        mixed.reshape(ys, 2, rows, width), residual, norm_gain.reshape(1, width), router.T, ids,
+        ssm_out, out_proj, residual, norm_gain.reshape(1, width), router.T, ids,
         gate_proj, up_proj, down_proj,
     )
 
@@ -438,13 +472,13 @@
     ssm_out = ssm_out.reshape(nodes, requests, columns)
     local_nodes = residual.shape[0]
     width = residual.shape[2]
-    mixed = jnp.einsum("jrk,kd->jrd", ssm_out, out_proj, preferred_element_type=jnp.float32)
     token_count = local_nodes * requests
     experts = router.shape[1]
     topk = expert_ids.shape[2]
     capacity = 2 * token_count * topk // (experts + experts // 4)
     layer_out = experts_block(
-        mixed,
+        ssm_out.reshape(nodes * requests, columns),
+        out_proj,
         residual.reshape(token_count, width),
         norm_gain,
         router,

time: 126 us -> 130 us (1.032)
  Pallas kernels: 101 us -> 111 us
  matrix products: 13 us -> 7.04 us
    pallas_call x1, Pallas kernels: 101 us -> 111 us  [experts_block(): pl.pallas_call(functools.partial(block_kernel, ys, zs, cap, chunks, backs...]
    dot_general x1 -> x0, matrix products: 5.99 us -> none  [body(): jnp.einsum('jrk,kd->jrd', ssm_out, out_proj, preferred_element_type=jnp.f...]
where the time goes in v3:
time: 130 us
  Pallas kernels  111 us (85%)
  matrix products  7.04 us (5%)
  blocking collectives  6.18 us (5%)
  local copies, waits for them, and re-layouts  4.3 us (3%)
  other arithmetic  1.63 us (1%)
    pallas_call x1, Pallas kernels, experts_block(): pl.pallas_call(functools.partial(block_kernel, ys, zs, cap, chunks, backs...  111 us
    all_gather x1, blocking collectives, body(): lax.all_gather(jnp.concatenate([write_vec, read_vec], axis=2), 'head', ax...  6.18 us
    dot_general x1, matrix products, body(): jnp.einsum('jrn,rhpn->jrhp', reads, cache_state, preferred_element_type=j...  3.35 us

profile of v3, /device:TPU:0, one launch (start us, length us, event | category | flops | bytes accessed | tf_op | source)
XLA Modules:
  0.0 129.8 jit_solution(10248480144561004169)
XLA Ops:
  0.0 0.7 pad_maximum_fusion
  0.7 1.0 convolution_convert_fusion.5
  1.7 1.0 fusion.6
  2.7 0.1 convolution_convert_fusion.3
  2.8 0.1 fusion.5
  3.0 0.3 convert_compare_fusion
  3.2 6.2 %all_gather.3 = bf16[16,8,256]{2,1,0:T(8,128)(2,1)S(1)} all-gather(bf16[4,8,256]{2,1,0:T(8,128)(2,1)S(1)} %pad_maximum_fusion), channel_id=1, replica_groups=mesh['groups'=2,'head'=4,'req'=4] {'head'}, dimensions={0}, use_global_device_ids=true | all-gather | bytes 81920 | tf_op jit(solution)/shard_map/all_gather | solution.py:449
  9.4 0.1 fusion.19
  9.5 0.9 negate_multiply_fusion
  10.4 0.2 fusion.14
  10.7 0.1 copy.33
  10.8 1.3 %reshape.34 = bf16[16,8,16,64]{3,2,1,0:T(8,128)(2,1)S(1)} reshape(bf16[16,8,1024]{2,1,0:T(8,128)(2,1)} %param.17) | data formatting | bytes 524288 | tf_op jit(solution)/shard_map/reshape | solution.py:451
  12.1 0.9 convolution_bitcast_fusion.1
  13.0 3.4 %fusion.3 = bf16[16,8,16,64]{3,0,2,1:T(8,128)(2,1)S(1)} fusion(f32[16,8,16,64]{3,0,2,1:T(8,128)S(1)} %convolution_bitcast_fusion.1, bf16[8,16,64,128]{3,2,1,0:T(8,128)(2,1)} %param.24, f32[16]{0:T(128)} %param.23, f32[16,8,16]{0,2,1:T(8,128)S(1)} %exponential_bitcast_fusion, bf16[16,8,16,64]{3,2,1,0:T(8,128)(2,1)S(1)} %reshape.34, ...), kind=kOutput, calls=%fused_computation.5 | convolution fusion | flops 34340864 | bytes 3186752 | tf_op jit(solution)/shard_map/jrn,rhpn->jrhp/dot_general | solution.py:465
  16.4 0.1 copy.36
  16.5 1.1 reshape_reshape.3.ssm
  17.6 110.5 %shard_map.163 = bf16[32,4096]{1,0:T(8,128)(2,1)} custom-call(bf16[128,1024]{1,0:T(8,128)(2,1)} %reshape_reshape.3.ssm, bf16[1024,4096]{1,0:T(8,128)(2,1)} %proj_h.1, bf16[32,4096]{1,0:T(8,128)(2,1)} %bitcast.41, f32[1,4096]{1,0:T(1,128)} %bitcast.43, bf16[64,4096]{1,0:T(8,128)(2,1)} %bitcast.40, s32[32,10]{1,0:T(8,128)} %bitcast.44, ...), custom_call_target="tpu_custom_call" | custom-call | tf_op jit(solution)/shard_map/pallas_call | solution.py:384
  128.1 1.7 %copy.54 = bf16[4,8,4096]{2,1,0:T(8,128)(2,1)} copy(bf16[4,8,4096]{2,1,0:T(8,128)(2,1)} %bitcast.39) | data formatting | bytes 524288
  (3 shorter events, 0.0 us)

commit v4 on v3

--- a/solution.py
+++ b/solution.py
@@ -87,12 +87,6 @@
 
     load_p(0).start()
     load_p(1).start()
-    for u in range(slots):
-        for cp in load_gu(jnp.int32(u)):
-            cp.start()
-    for k in range(dslots):
-        load_d(k).start()
-
     barrier = pltpu.get_barrier_semaphore()
     pl.semaphore_signal(barrier, inc=1, device_id={"head": twin, "req": z}, device_id_type=pl.DeviceIdType.MESH)
     for d in range(1, ys):
@@ -126,6 +120,11 @@
         mixer(k)
         if k > 0:
             mixer_y(k - 1)
+    for u in range(slots):
+        for cp in load_gu(jnp.int32(u)):
+            cp.start()
+    for k in range(dslots):
+        load_d(k).start()
     mixer_y(chunks - 1)
     sums = []
     for k in range(chunks):
@@ -345,9 +344,9 @@
 
     for k in range(backs):
         produce(k)
-        if k < 2:
+        if k == 0:
             sum_twin(k)
-        elif k > 2:
+        elif k > 1:
             sum_twin(k - 1)
         if k >= 4:
             sum_y(k - 4)
@@ -356,7 +355,8 @@
     sum_twin(backs - 1)
     for k in range(backs - 4, backs):
         sum_y(k)
-        finish(k - 2)
+        if k >= 2:
+            finish(k - 2)
     finish(backs - 2)
     finish(backs - 1)
     for cp in pending:
@@ -370,9 +370,9 @@
     rows, width = residual.shape
     held, _, hidden = gate_proj.shape
     chunks = 4
-    backs = 8
+    backs = 4
     slots = min(8, held * chunks)
-    dslots = 4
+    dslots = 2
     cw = width // chunks
     rw = width // backs
     blocks = heads * zs
@@ -446,7 +446,14 @@
     heads = step_raw.shape[2]
     head_size = columns // heads
     state = write_vec.shape[2]
-    both = lax.all_gather(jnp.concatenate([write_vec, read_vec], axis=2), "head", axis=0, tiled=True)
+    own = jnp.concatenate([write_vec, read_vec], axis=2)
+    count = lax.axis_size("head")
+    turned = [own] + [
+        lax.ppermute(own, "head", [(i, (i + d) % count) for i in range(count)]) for d in range(1, count)
+    ]
+    ring = jnp.concatenate(turned[::-1] * 2, axis=0)
+    start = (count - 1 - lax.axis_index("head")) * own.shape[0]
+    both = lax.dynamic_slice_in_dim(ring, start, count * own.shape[0], axis=0)
     writes, reads = both[:, :, :state], both[:, :, state:]
     inputs4 = ssm_input.reshape(nodes, requests, heads, head_size)
     step = jax.nn.softplus(step_raw + step_bias)

time: 130 us -> 119 us (0.915)
  Pallas kernels: 111 us -> 100 us
  blocking collectives: 6.18 us -> 0 us
  starting transfers between devices: 0 us -> 4.43 us
  local copies, waits for them, and re-layouts: 4.3 us -> 5.84 us
    pallas_call x1, Pallas kernels: 111 us -> 100 us  [experts_block(): pl.pallas_call(functools.partial(block_kernel, ys, zs, cap, chunks, backs...]
    all_gather x1 -> x0, blocking collectives: 6.18 us -> none  [body(): lax.all_gather(jnp.concatenate([write_vec, read_vec], axis=2), 'head', ax...]
    ppermute x0 -> x3, starting transfers between devices: none -> 4.43 us  [body(): lax.ppermute(own, 'head', [(i, (i + d) % count) for i in range(count)])]
  transfers between devices with their start and end apart: 0 -> 3, of which waited for: 0 -> 0; matrix products, arithmetic and copies ran while one was open for 0% -> 4% of each run, Pallas kernels for 0% -> 0%
where the time goes in v4:
time: 119 us
  Pallas kernels  100 us (84%)
  matrix products  7.18 us (6%)
  local copies, waits for them, and re-layouts  5.84 us (5%)
  starting transfers between devices  4.43 us (4%)
    pallas_call x1, Pallas kernels, experts_block(): pl.pallas_call(functools.partial(block_kernel, ys, zs, cap, chunks, backs...  100 us
    ppermute x3, starting transfers between devices, body(): lax.ppermute(own, 'head', [(i, (i + d) % count) for i in range(count)])  4.43 us
    dot_general x1, matrix products, body(): jnp.einsum('jrn,rhpn->jrhp', reads, cache_state, preferred_element_type=j...  3.39 us
  transfers between devices with their start and end apart: 3, of which 0 were waited for; matrix products, arithmetic and copies ran while one was open for 4% of the time, Pallas kernels for 0%

profile of v4, /device:TPU:0, one launch (start us, length us, event | category | flops | bytes accessed | tf_op | source)
XLA Modules:
  0.0 118.7 jit_solution(13874776234503526900)
XLA Ops:
  0.0 0.7 copy_dynamic-update-slice_fusion.1
  0.7 0.7 copy_dynamic-update-slice_fusion
  1.4 0.5 collective-permute-start.2
  1.9 2.6 %collective-permute-start.1 = (bf16[4,8,256]{2,0,1:T(4,128)(2,1)S(1)}, bf16[4,8,256]{2,0,1:T(4,128)(2,1)S(1)}, u32[]{:S(2)}, u32[]{:S(2)}) collective-permute-start(bf16[4,8,256]{2,0,1:T(4,128)(2,1)S(1)} %copy_dynamic-update-slice_fusion), channel_id=1, source_target_pairs={{0,8},{4,12},{8,0},{12,4},{1,9},{5,13},{9,1},{13,5},{2,10},{6,14},... | collective-permute-start | bytes 49160 | tf_op jit(solution)/shard_map/ppermute | solution.py:452
  4.4 1.4 %collective-permute-start = (bf16[4,8,256]{2,0,1:T(4,128)(2,1)S(1)}, bf16[4,8,256]{2,0,1:T(4,128)(2,1)S(1)}, u32[]{:S(2)}, u32[]{:S(2)}) collective-permute-start(bf16[4,8,256]{2,0,1:T(4,128)(2,1)S(1)} %copy_dynamic-update-slice_fusion), channel_id=1, source_target_pairs={{0,12},{4,0},{8,4},{12,8},{1,13},{5,1},{9,5},{13,9},{2,14},{6,2},{... | collective-permute-start | bytes 49160 | tf_op jit(solution)/shard_map/ppermute | solution.py:452
  5.8 1.0 convolution_convert_fusion.5
  6.8 0.1 convolution_convert_fusion.3
  7.0 1.0 fusion.6
  7.9 0.1 fusion.5
  8.1 0.3 convert_compare_fusion
  8.3 0.9 negate_multiply_fusion
  9.2 0.2 fusion.14
  9.5 0.1 copy.26
  9.6 1.3 %reshape.34 = bf16[16,8,16,64]{3,2,1,0:T(8,128)(2,1)S(1)} reshape(bf16[16,8,1024]{2,1,0:T(8,128)(2,1)} %param.17) | data formatting | bytes 524288 | tf_op jit(solution)/shard_map/reshape | solution.py:458
  10.9 0.0 collective-permute-done.2
  11.0 0.0 collective-permute-done.1
  11.0 0.0 collective-permute-done
  11.0 0.1 concatenate.7
  11.1 0.2 fusion.19
  11.3 0.9 convolution_bitcast_fusion.1
  12.2 3.4 %fusion.3 = bf16[16,8,16,64]{3,0,2,1:T(8,128)(2,1)S(1)} fusion(f32[16,8,16,64]{3,0,2,1:T(8,128)S(1)} %convolution_bitcast_fusion.1, bf16[8,16,64,128]{3,2,1,0:T(8,128)(2,1)} %param.24, f32[16]{0:T(128)} %param.23, f32[16,8,16]{0,2,1:T(8,128)S(1)} %exponential_bitcast_fusion, bf16[16,8,16,64]{3,2,1,0:T(8,128)(2,1)S(1)} %reshape.34, ...), kind=kOutput, calls=%fused_computation.5 | convolution fusion | flops 34340864 | bytes 4030536 | tf_op jit(solution)/shard_map/jrn,rhpn->jrhp/dot_general | solution.py:472
  15.6 0.1 copy.29
  15.7 1.1 reshape_reshape.3.ssm
  16.8 100.3 %shard_map.163 = bf16[32,4096]{1,0:T(8,128)(2,1)} custom-call(bf16[128,1024]{1,0:T(8,128)(2,1)} %reshape_reshape.3.ssm, bf16[1024,4096]{1,0:T(8,128)(2,1)} %proj_h.1, bf16[32,4096]{1,0:T(8,128)(2,1)} %bitcast.41, f32[1,4096]{1,0:T(1,128)} %bitcast.43, bf16[64,4096]{1,0:T(8,128)(2,1)} %bitcast.40, s32[32,10]{1,0:T(8,128)} %bitcast.44, ...), custom_call_target="tpu_custom_call" | custom-call | tf_op jit(solution)/shard_map/pallas_call | solution.py:384
  117.1 1.7 %copy.40 = bf16[4,8,4096]{2,1,0:T(8,128)(2,1)} copy(bf16[4,8,4096]{2,1,0:T(8,128)(2,1)} %bitcast.39) | data formatting | bytes 524288
  (2 shorter events, 0.0 us)
Async XLA Ops:
  1.4 9.5 %collective-permute-start.2 = (bf16[4,8,256]{2,0,1:T(4,128)(2,1)S(1)}, bf16[4,8,256]{2,0,1:T(4,128)(2,1)S(1)}, u32[]{:S(2)}, u32[]{:S(2)}) collective-permute-start(bf16[4,8,256]{2,0,1:T(4,128)(2,1)S(1)} %copy_dynamic-update-slice_fusion), channel_id=1, source_target_pairs={{0,4},{4,8},{8,12},{12,0},{1,5},{5,9},{9,13},{13,1},{2,6},{6,10},{... | collective-permute-start | bytes 49160 | tf_op jit(solution)/shard_map/ppermute | solution.py:452
  1.9 9.1 %collective-permute-start.1 = (bf16[4,8,256]{2,0,1:T(4,128)(2,1)S(1)}, bf16[4,8,256]{2,0,1:T(4,128)(2,1)S(1)}, u32[]{:S(2)}, u32[]{:S(2)}) collective-permute-start(bf16[4,8,256]{2,0,1:T(4,128)(2,1)S(1)} %copy_dynamic-update-slice_fusion), channel_id=1, source_target_pairs={{0,8},{4,12},{8,0},{12,4},{1,9},{5,13},{9,1},{13,5},{2,10},{6,14},... | collective-permute-start | bytes 49160 | tf_op jit(solution)/shard_map/ppermute | solution.py:452
  4.4 6.5 %collective-permute-start = (bf16[4,8,256]{2,0,1:T(4,128)(2,1)S(1)}, bf16[4,8,256]{2,0,1:T(4,128)(2,1)S(1)}, u32[]{:S(2)}, u32[]{:S(2)}) collective-permute-start(bf16[4,8,256]{2,0,1:T(4,128)(2,1)S(1)} %copy_dynamic-update-slice_fusion), channel_id=1, source_target_pairs={{0,12},{4,0},{8,4},{12,8},{1,13},{5,1},{9,5},{13,9},{2,14},{6,2},{... | collective-permute-start | bytes 49160 | tf_op jit(solution)/shard_map/ppermute | solution.py:452

commit v5 on v4

--- a/solution.py
+++ b/solution.py
@@ -243,6 +243,7 @@
     relay_z(0)
     relay_y(0)
     all_in(0)
+    relay_z(1)
 
     gates = buf0[:, :, cw:].reshape(tokens, 128)
     first = ((head * zs + z) * held) % experts
@@ -265,7 +266,6 @@
     for h in range(held):
         smat[h * cap : (h + 1) * cap, :] = jnp.where(rankt[h : h + 1, :] == slot_row, 1.0, 0.0).astype(BF16)
     select(0)
-    relay_z(1)
     slot_lane = lax.broadcasted_iota(jnp.int32, (tokens, cap), 1).astype(F32)
     for h in range(held):
         col = jnp.where(rank[:, h : h + 1] == slot_lane, g[:, h : h + 1], 0.0).astype(BF16)

time: 119 us -> 116 us (0.975)
  Pallas kernels: 100 us -> 96.8 us
    pallas_call x1, Pallas kernels: 100 us -> 96.8 us  [experts_block(): pl.pallas_call(functools.partial(block_kernel, ys, zs, cap, chunks, backs...]
where the time goes in v5:
time: 116 us; the launch traced here: 115 us
  Pallas kernels  96.8 us (83%)
  matrix products  7.18 us (6%)
  local copies, waits for them, and re-layouts  5.84 us (5%)
  starting transfers between devices  4.43 us (4%)
    pallas_call x1, Pallas kernels, experts_block(): pl.pallas_call(functools.partial(block_kernel, ys, zs, cap, chunks, backs...  96.8 us
    ppermute x3, starting transfers between devices, body(): lax.ppermute(own, 'head', [(i, (i + d) % count) for i in range(count)])  4.43 us
    dot_general x1, matrix products, body(): jnp.einsum('jrn,rhpn->jrhp', reads, cache_state, preferred_element_type=j...  3.39 us
    unnamed x2, local copies, waits for them, and re-layouts  2.37 us
  transfers between devices with their start and end apart: 3, of which 0 were waited for; matrix products, arithmetic and copies ran while one was open for 4% of the time, Pallas kernels for 0%

profile of v5, /device:TPU:0, one launch (start us, length us, event | category | flops | bytes accessed | tf_op | source)
XLA Modules:
  0.0 115.2 jit_solution(265617706797663422)
XLA Ops:
  0.0 0.7 copy_dynamic-update-slice_fusion.1
  0.7 0.7 copy_dynamic-update-slice_fusion
  1.4 0.5 collective-permute-start.2
  1.9 2.6 %collective-permute-start.1 = (bf16[4,8,256]{2,0,1:T(4,128)(2,1)S(1)}, bf16[4,8,256]{2,0,1:T(4,128)(2,1)S(1)}, u32[]{:S(2)}, u32[]{:S(2)}) collective-permute-start(bf16[4,8,256]{2,0,1:T(4,128)(2,1)S(1)} %copy_dynamic-update-slice_fusion), channel_id=1, source_target_pairs={{0,8},{4,12},{8,0},{12,4},{1,9},{5,13},{9,1},{13,5},{2,10},{6,14},... | collective-permute-start | bytes 49160 | tf_op jit(solution)/shard_map/ppermute | solution.py:452
  4.4 1.4 %collective-permute-start = (bf16[4,8,256]{2,0,1:T(4,128)(2,1)S(1)}, bf16[4,8,256]{2,0,1:T(4,128)(2,1)S(1)}, u32[]{:S(2)}, u32[]{:S(2)}) collective-permute-start(bf16[4,8,256]{2,0,1:T(4,128)(2,1)S(1)} %copy_dynamic-update-slice_fusion), channel_id=1, source_target_pairs={{0,12},{4,0},{8,4},{12,8},{1,13},{5,1},{9,5},{13,9},{2,14},{6,2},{... | collective-permute-start | bytes 49160 | tf_op jit(solution)/shard_map/ppermute | solution.py:452
  5.8 1.0 convolution_convert_fusion.5
  6.8 0.1 convolution_convert_fusion.3
  7.0 1.0 fusion.6
  7.9 0.1 fusion.5
  8.1 0.3 convert_compare_fusion
  8.3 0.9 negate_multiply_fusion
  9.2 0.2 fusion.14
  9.5 0.1 copy.26
  9.6 1.3 %reshape.34 = bf16[16,8,16,64]{3,2,1,0:T(8,128)(2,1)S(1)} reshape(bf16[16,8,1024]{2,1,0:T(8,128)(2,1)} %param.17) | data formatting | bytes 524288 | tf_op jit(solution)/shard_map/reshape | solution.py:458
  10.9 0.0 collective-permute-done.2
  11.0 0.0 collective-permute-done.1
  11.0 0.0 collective-permute-done
  11.0 0.1 concatenate.7
  11.1 0.2 fusion.19
  11.3 0.9 convolution_bitcast_fusion.1
  12.2 3.4 %fusion.3 = bf16[16,8,16,64]{3,0,2,1:T(8,128)(2,1)S(1)} fusion(f32[16,8,16,64]{3,0,2,1:T(8,128)S(1)} %convolution_bitcast_fusion.1, bf16[8,16,64,128]{3,2,1,0:T(8,128)(2,1)} %param.24, f32[16]{0:T(128)} %param.23, f32[16,8,16]{0,2,1:T(8,128)S(1)} %exponential_bitcast_fusion, bf16[16,8,16,64]{3,2,1,0:T(8,128)(2,1)S(1)} %reshape.34, ...), kind=kOutput, calls=%fused_computation.5 | convolution fusion | flops 34340864 | bytes 4030536 | tf_op jit(solution)/shard_map/jrn,rhpn->jrhp/dot_general | solution.py:472
  15.6 0.1 copy.29
  15.7 1.1 reshape_reshape.3.ssm
  16.8 96.8 %shard_map.163 = bf16[32,4096]{1,0:T(8,128)(2,1)} custom-call(bf16[128,1024]{1,0:T(8,128)(2,1)} %reshape_reshape.3.ssm, bf16[1024,4096]{1,0:T(8,128)(2,1)} %proj_h.1, bf16[32,4096]{1,0:T(8,128)(2,1)} %bitcast.41, f32[1,4096]{1,0:T(1,128)} %bitcast.43, bf16[64,4096]{1,0:T(8,128)(2,1)} %bitcast.40, s32[32,10]{1,0:T(8,128)} %bitcast.44, ...), custom_call_target="tpu_custom_call" | custom-call | tf_op jit(solution)/shard_map/pallas_call | solution.py:384
  113.6 1.7 %copy.40 = bf16[4,8,4096]{2,1,0:T(8,128)(2,1)} copy(bf16[4,8,4096]{2,1,0:T(8,128)(2,1)} %bitcast.39) | data formatting | bytes 524288
  (2 shorter events, 0.0 us)
Async XLA Ops:
  1.4 9.5 %collective-permute-start.2 = (bf16[4,8,256]{2,0,1:T(4,128)(2,1)S(1)}, bf16[4,8,256]{2,0,1:T(4,128)(2,1)S(1)}, u32[]{:S(2)}, u32[]{:S(2)}) collective-permute-start(bf16[4,8,256]{2,0,1:T(4,128)(2,1)S(1)} %copy_dynamic-update-slice_fusion), channel_id=1, source_target_pairs={{0,4},{4,8},{8,12},{12,0},{1,5},{5,9},{9,13},{13,1},{2,6},{6,10},{... | collective-permute-start | bytes 49160 | tf_op jit(solution)/shard_map/ppermute | solution.py:452
  1.9 9.1 %collective-permute-start.1 = (bf16[4,8,256]{2,0,1:T(4,128)(2,1)S(1)}, bf16[4,8,256]{2,0,1:T(4,128)(2,1)S(1)}, u32[]{:S(2)}, u32[]{:S(2)}) collective-permute-start(bf16[4,8,256]{2,0,1:T(4,128)(2,1)S(1)} %copy_dynamic-update-slice_fusion), channel_id=1, source_target_pairs={{0,8},{4,12},{8,0},{12,4},{1,9},{5,13},{9,1},{13,5},{2,10},{6,14},... | collective-permute-start | bytes 49160 | tf_op jit(solution)/shard_map/ppermute | solution.py:452
  4.4 6.5 %collective-permute-start = (bf16[4,8,256]{2,0,1:T(4,128)(2,1)S(1)}, bf16[4,8,256]{2,0,1:T(4,128)(2,1)S(1)}, u32[]{:S(2)}, u32[]{:S(2)}) collective-permute-start(bf16[4,8,256]{2,0,1:T(4,128)(2,1)S(1)} %copy_dynamic-update-slice_fusion), channel_id=1, source_target_pairs={{0,12},{4,0},{8,4},{12,8},{1,13},{5,1},{9,5},{13,9},{2,14},{6,2},{... | collective-permute-start | bytes 49160 | tf_op jit(solution)/shard_map/ppermute | solution.py:452
